TPU v7x, 32 devices: a whole 2x2x4 slice. The times are simulated.
32 devices in a mesh: ctx: 8 (over y, x, core), wa: 4 (over z).
Axes of the slice: x: 2, y: 2, z: 4, core: 2. Of those that a mesh axis runs over, the one named last changes fastest.
Arguments:
- tokens: bfloat16 [8, 1024, 768], P('wa', 'ctx'), may hold values from -6 to 6
- doc_lengths: int32 [8], replicated, may hold values from 256 to 1024, as said below
- group_deal: int32 [8, 8], replicated, may hold values from 0 to 7, each once within a row
- qkv_weight: bfloat16 [768, 2304], P('wa'), may hold values from -0.21875 to 0.21875
- out_weight: bfloat16 [768, 768], P('wa'), may hold values from -2.5 to 2.5
- up_weight: bfloat16 [768, 3072], P('wa'), may hold values from -0.21875 to 0.21875
- up_bias: bfloat16 [3072], P('wa'), may hold values from -3 to 3
- down_weight: bfloat16 [3072, 768], P('wa'), may hold values from -0.109375 to 0.109375
- proj_weight: bfloat16 [768, 128], P('wa'), may hold values from -0.21875 to 0.21875
- vectors: bfloat16 [8, 768], P(None, 'wa'), may hold values from -2 to 2
- cotangent: bfloat16 [8, 1024, 128], P('wa', 'ctx'), may hold values from -6 to 6
Outputs:
- embeddings: bfloat16 [8, 1024, 128], P('wa', 'ctx')
- tokens_grad: float32 [8, 1024, 768], P('wa', 'ctx')
- qkv_grad: float32 [768, 2304], P('wa')
- out_grad: float32 [768, 768], P('wa')
- up_grad: float32 [768, 3072], P('wa')
- bias_grad: float32 [3072], P('wa')
- down_grad: float32 [3072, 768], P('wa')
- proj_grad: float32 [768, 128], P('wa')
- vectors_grad: float32 [8, 768], P(None, 'wa')
Inputs may be any that keep to these rules, and one draw needn't show every extreme that they name: `doc_lengths`: every draw has a sequence with all 1024 slots valid. `group_deal`: each row is a permutation of the block numbers of a sequence.
All inputs are finite; a program needn't handle non-finite values.
Results may differ from a plain program's by a relative error of at most 0.023.
Values may be sent and summed in bfloat16 or wider, within the bound.
No kernel may reach another device: no remote copies, remote signals or barrier semaphores. Data moves between devices by JAX's collectives and lax.ppermute only.
A program may use at most 256 MiB of HBM per device.

v0:
```python
from functools import partial

import jax
import jax.numpy as jnp
from jax import lax
from jax.experimental import pallas as pl
from jax.experimental.pallas import tpu as pltpu
from jax.sharding import PartitionSpec as P

H = 12
HEAD = 64


NEG_FILL = -1e30
NORM_EPS = 1e-06
ROOT_HALF = 0.7071067811865476
DENSITY_SCALE = 0.3989422804014327


def norm_rows(inputs, gain_row, shift_row):
    middle = jnp.mean(inputs, axis=-1, keepdims=True)
    center = inputs - middle
    spread = jnp.mean(center * center, axis=-1, keepdims=True)
    scaled = lax.rsqrt(spread + NORM_EPS)
    unit_rows = center * scaled
    return (unit_rows * gain_row + shift_row, unit_rows, scaled)


def norm_back(grad_in, unit_rows, scaled, gain_row):
    gain_grad = jnp.sum(grad_in * unit_rows, axis=(0, 1))
    shift_grad = jnp.sum(grad_in, axis=(0, 1))
    inner_grad = grad_in * gain_row
    centered = inner_grad - jnp.mean(inner_grad, axis=-1, keepdims=True)
    result = scaled * (
        centered - unit_rows * jnp.mean(inner_grad * unit_rows, axis=-1, keepdims=True)
    )
    return (result, gain_grad, shift_grad)


def gelu_both(inner_sum):
    normal_cdf = 0.5 * (1.0 + lax.erf(inner_sum * ROOT_HALF))
    density = jnp.exp(-0.5 * inner_sum * inner_sum) * DENSITY_SCALE
    return (inner_sum * normal_cdf, normal_cdf + inner_sum * density)


def split_tiles(key_rows, value_rows, key_valid):
    key_count = key_rows.shape[0]
    tile_width = 512
    tile_count = key_count // tile_width
    return (
        key_rows.reshape(tile_count, tile_width, H, HEAD),
        value_rows.reshape(tile_count, tile_width, H, HEAD),
        key_valid.reshape(tile_count, tile_width),
    )


def masked_scores(queries, key_tile, mask_tile):
    products = jnp.einsum("qhd,khd->hqk", queries, key_tile, preferred_element_type=jnp.float32)
    return jnp.where(mask_tile[None, None, :], products, NEG_FILL)


def attend_forward(queries, key_rows, value_rows, key_valid):
    key_tiles, value_tiles, mask_tiles = split_tiles(key_rows, value_rows, key_valid)
    row_span = queries.shape[0]

    def stats_step(running, portion):
        highest, summed = running
        key_tile, mask_tile = portion
        scores = masked_scores(queries, key_tile, mask_tile)
        new_peak = jnp.maximum(highest, jnp.max(scores, axis=-1))
        raised = jnp.where(mask_tile[None, None, :], jnp.exp(scores - new_peak[:, :, None]), 0.0)
        return ((new_peak, summed * jnp.exp(highest - new_peak) + jnp.sum(raised, axis=-1)), None)

    start_peak = jnp.full((H, row_span), NEG_FILL, jnp.float32)
    start_sum = jnp.zeros((H, row_span), jnp.float32)
    (highest, summed), _ = lax.scan(stats_step, (start_peak, start_sum), (key_tiles, mask_tiles))
    logsum = highest + jnp.log(summed)

    def value_step(running, portion):
        key_tile, value_tile, mask_tile = portion
        scores = masked_scores(queries, key_tile, mask_tile)
        prob_low = jnp.where(
            mask_tile[None, None, :], jnp.exp(scores - logsum[:, :, None]), 0.0
        ).astype(jnp.bfloat16)
        return (
            running
            + jnp.einsum("hqk,khd->qhd", prob_low, value_tile, preferred_element_type=jnp.float32),
            None,
        )

    attended, _ = lax.scan(
        value_step,
        jnp.zeros((row_span, H, HEAD), jnp.float32),
        (key_tiles, value_tiles, mask_tiles),
    )
    return (attended, logsum)


def attend_backward(
    queries, key_rows, value_rows, key_valid, logsum, delta_rows, grad_heads, with_keys
):
    key_tiles, value_tiles, mask_tiles = split_tiles(key_rows, value_rows, key_valid)

    def back_step(running, portion):
        key_tile, value_tile, mask_tile = portion
        scores = masked_scores(queries, key_tile, mask_tile)
        prob_rows = jnp.where(mask_tile[None, None, :], jnp.exp(scores - logsum[:, :, None]), 0.0)
        prob_grad = jnp.einsum(
            "qhd,khd->hqk", grad_heads, value_tile, preferred_element_type=jnp.float32
        )
        score_low = (prob_rows * (prob_grad - delta_rows[:, :, None])).astype(jnp.bfloat16)
        running = running + jnp.einsum(
            "hqk,khd->qhd", score_low, key_tile, preferred_element_type=jnp.float32
        )
        value_part = jnp.einsum(
            "hqk,qhd->khd",
            prob_rows.astype(jnp.bfloat16),
            grad_heads,
            preferred_element_type=jnp.float32,
        )
        key_part = jnp.einsum(
            "hqk,qhd->khd", score_low, queries, preferred_element_type=jnp.float32
        )
        return (running, (key_part, value_part))

    start_grad = jnp.zeros(queries.shape, jnp.float32)
    query_grad, pieces = lax.scan(back_step, start_grad, (key_tiles, value_tiles, mask_tiles))
    key_count = key_rows.shape[0]
    return (
        query_grad,
        pieces[0].reshape(key_count, H * HEAD),
        pieces[1].reshape(key_count, H * HEAD),
    )


def general_body(
    tokens,
    doc_lengths,
    group_deal,
    qkv_weight,
    out_weight,
    up_weight,
    up_bias,
    down_weight,
    proj_weight,
    vectors,
    cotangent,
):
    gathered = (
        lax.all_gather(qkv_weight, "wa", axis=0, tiled=True),
        lax.all_gather(out_weight, "wa", axis=0, tiled=True),
        lax.all_gather(up_weight, "wa", axis=0, tiled=True),
        lax.all_gather(up_bias, "wa", axis=0, tiled=True),
        lax.all_gather(down_weight, "wa", axis=0, tiled=True),
        lax.all_gather(proj_weight, "wa", axis=0, tiled=True),
        lax.all_gather(vectors, "wa", axis=1, tiled=True),
    )
    qkv_full, out_full, up_full, bias_full, down_full, proj_full, vector_full = gathered
    seq_count, group_rows, model_width = tokens.shape
    ctx_count = lax.axis_size("ctx")
    seq_start = lax.axis_index("wa") * seq_count
    my_lengths = lax.dynamic_slice_in_dim(doc_lengths, seq_start, seq_count, 0)
    my_deal = lax.dynamic_slice_in_dim(group_deal, seq_start, seq_count, 0)
    offsets = jnp.tile(jnp.arange(group_rows, dtype=jnp.int32), ctx_count)
    positions = jnp.repeat(my_deal, group_rows, axis=1) * group_rows + offsets[None, :]
    key_valid = positions < my_lengths[:, None]
    query_valid = lax.dynamic_slice_in_dim(
        key_valid, lax.axis_index("ctx") * group_rows, group_rows, 1
    )
    row_mask = query_valid.astype(jnp.float32)[:, :, None]
    query_scale = HEAD ** (-0.5)
    mixed_rows = jnp.einsum("scd,de->sce", tokens, qkv_full, preferred_element_type=jnp.float32)
    queries = ((mixed_rows[:, :, :model_width] + vector_full[0]) * query_scale).astype(jnp.bfloat16)
    key_rows = mixed_rows[:, :, model_width : 2 * model_width].astype(jnp.bfloat16)
    value_rows = (mixed_rows[:, :, 2 * model_width :] + vector_full[1]).astype(jnp.bfloat16)
    all_keys, all_values = (
        lax.all_gather(key_rows, "ctx", axis=1, tiled=True),
        lax.all_gather(value_rows, "ctx", axis=1, tiled=True),
    )
    query_heads = queries.reshape(seq_count, group_rows, H, HEAD)
    attended, logsum = jax.vmap(attend_forward)(query_heads, all_keys, all_values, key_valid)
    attended_low = attended.reshape(seq_count, group_rows, model_width).astype(jnp.bfloat16)
    first_sum = tokens.astype(jnp.float32) + (
        jnp.einsum("scd,de->sce", attended_low, out_full, preferred_element_type=jnp.float32)
        + vector_full[2]
    )
    normed, unit_one, scale_one = norm_rows(first_sum, vector_full[3], vector_full[4])
    normed_low = normed.astype(jnp.bfloat16)
    inner_sum = (
        jnp.einsum("scd,df->scf", normed_low, up_full, preferred_element_type=jnp.float32)
        + bias_full
    )
    active, gelu_slope = gelu_both(inner_sum)
    active_low = active.astype(jnp.bfloat16)
    second_sum = normed + (
        jnp.einsum("scf,fd->scd", active_low, down_full, preferred_element_type=jnp.float32)
        + vector_full[5]
    )
    final_sum, unit_two, scale_two = norm_rows(second_sum, vector_full[6], vector_full[7])
    final_low = final_sum.astype(jnp.bfloat16)
    project = jnp.einsum("scd,de->sce", final_low, proj_full, preferred_element_type=jnp.float32)
    inverse = lax.rsqrt(jnp.sum(project * project, axis=-1, keepdims=True) + NORM_EPS)
    direction = project * inverse
    embeddings = (direction * row_mask).astype(jnp.bfloat16)
    upstream = cotangent.astype(jnp.float32) * row_mask
    project_grad = (
        inverse * (upstream - direction * jnp.sum(upstream * direction, axis=-1, keepdims=True))
    ).astype(jnp.bfloat16)
    proj_grad = jnp.einsum(
        "scd,sce->de", final_low, project_grad, preferred_element_type=jnp.float32
    )
    final_grad = jnp.einsum(
        "sce,de->scd", project_grad, proj_full, preferred_element_type=jnp.float32
    )
    second_grad, gain_two, shift_two = norm_back(final_grad, unit_two, scale_two, vector_full[6])
    down_low = second_grad.astype(jnp.bfloat16)
    down_grad = jnp.einsum("scf,scd->fd", active_low, down_low, preferred_element_type=jnp.float32)
    inner_grad = (
        jnp.einsum("scd,fd->scf", down_low, down_full, preferred_element_type=jnp.float32)
        * gelu_slope
    )
    bias_grad = jnp.sum(inner_grad, axis=(0, 1))
    inner_low = inner_grad.astype(jnp.bfloat16)
    up_grad = jnp.einsum("scd,scf->df", normed_low, inner_low, preferred_element_type=jnp.float32)
    normed_grad = second_grad + jnp.einsum(
        "scf,df->scd", inner_low, up_full, preferred_element_type=jnp.float32
    )
    first_grad, gain_one, shift_one = norm_back(normed_grad, unit_one, scale_one, vector_full[3])
    first_low = first_grad.astype(jnp.bfloat16)
    out_grad = jnp.einsum(
        "scd,sce->de", attended_low, first_low, preferred_element_type=jnp.float32
    )
    attended_grad = jnp.einsum(
        "sce,de->scd", first_low, out_full, preferred_element_type=jnp.float32
    ).astype(jnp.bfloat16)
    grad_heads = attended_grad.reshape(seq_count, group_rows, H, HEAD)
    delta_rows = jnp.sum(grad_heads.astype(jnp.float32) * attended, axis=-1)
    delta_heads = jnp.swapaxes(delta_rows, 1, 2)
    query_grad, key_terms, value_terms = jax.vmap(partial(attend_backward, with_keys=True))(
        query_heads, all_keys, all_values, key_valid, logsum, delta_heads, grad_heads
    )
    key_grad, value_grad = (
        lax.psum_scatter(
            key_terms.astype(jnp.bfloat16), "ctx", scatter_dimension=1, tiled=True
        ).astype(jnp.float32),
        lax.psum_scatter(
            value_terms.astype(jnp.bfloat16), "ctx", scatter_dimension=1, tiled=True
        ).astype(jnp.float32),
    )
    query_part = (
        query_grad.reshape(seq_count, group_rows, model_width).astype(jnp.bfloat16) * query_scale
    )
    value_part = value_grad.astype(jnp.bfloat16)
    mixed_grad = jnp.concatenate([query_part, key_grad.astype(jnp.bfloat16), value_part], axis=-1)
    qkv_grad = jnp.einsum("scd,sce->de", tokens, mixed_grad, preferred_element_type=jnp.float32)
    tokens_grad = first_grad + jnp.einsum(
        "sce,de->scd", mixed_grad, qkv_full, preferred_element_type=jnp.float32
    )
    vectors_grad = jnp.stack(
        [
            jnp.sum(query_part.astype(jnp.float32), axis=(0, 1)),
            jnp.sum(value_part.astype(jnp.float32), axis=(0, 1)),
            jnp.sum(first_grad, axis=(0, 1)),
            gain_one,
            shift_one,
            jnp.sum(second_grad, axis=(0, 1)),
            gain_two,
            shift_two,
        ],
        axis=0,
    )
    owned = (
        lax.psum_scatter(
            qkv_grad.astype(jnp.bfloat16), "wa", scatter_dimension=0, tiled=True
        ).astype(jnp.float32),
        lax.psum_scatter(
            out_grad.astype(jnp.bfloat16), "wa", scatter_dimension=0, tiled=True
        ).astype(jnp.float32),
        lax.psum_scatter(
            up_grad.astype(jnp.bfloat16), "wa", scatter_dimension=0, tiled=True
        ).astype(jnp.float32),
        lax.psum_scatter(
            bias_grad.astype(jnp.bfloat16), "wa", scatter_dimension=0, tiled=True
        ).astype(jnp.float32),
        lax.psum_scatter(
            down_grad.astype(jnp.bfloat16), "wa", scatter_dimension=0, tiled=True
        ).astype(jnp.float32),
        lax.psum_scatter(
            proj_grad.astype(jnp.bfloat16), "wa", scatter_dimension=0, tiled=True
        ).astype(jnp.float32),
        lax.psum_scatter(
            vectors_grad.astype(jnp.bfloat16), "wa", scatter_dimension=1, tiled=True
        ).astype(jnp.float32),
    )
    summed = (
        lax.psum(owned[0].astype(jnp.bfloat16), "ctx").astype(jnp.float32),
        lax.psum(owned[1].astype(jnp.bfloat16), "ctx").astype(jnp.float32),
        lax.psum(owned[2].astype(jnp.bfloat16), "ctx").astype(jnp.float32),
        lax.psum(owned[3].astype(jnp.bfloat16), "ctx").astype(jnp.float32),
        lax.psum(owned[4].astype(jnp.bfloat16), "ctx").astype(jnp.float32),
        lax.psum(owned[5].astype(jnp.bfloat16), "ctx").astype(jnp.float32),
        lax.psum(owned[6].astype(jnp.bfloat16), "ctx").astype(jnp.float32),
    )
    return (
        embeddings,
        tokens_grad,
        summed[0],
        summed[1],
        summed[2],
        summed[3],
        summed[4],
        summed[5],
        summed[6],
    )


PLANE = 8
LINE = 4
SPAN = 128
OWN = 2 * SPAN
WIDTH = H * HEAD
INNER = 4 * WIDTH
SHARD = WIDTH // LINE
HALF = SHARD // 2
PIECE = INNER // LINE // PLANE
SLICE = LINE * PIECE
HEADS = 3
WIDE = HEADS * HEAD
PAD = 256
SLOTS = PLANE * SPAN
BLOCK = SHARD // 4
FIRST = SHARD + BLOCK
SIDE = PIECE + 16
PARTS = FIRST + 2 * SIDE
QUARTER = HALF // 2
COLS = HALF + QUARTER
EMBED = 128
ORDER = (0, 4, 2, 6, 1, 5, 3, 7)
NEAR = (0, 2, 1, 3)
F32 = jnp.float32
BF16 = jnp.bfloat16

NN = ((1,), (0,))
NT = ((1,), (1,))
TN = ((0,), (0,))


def dot(left, right, dims):
    return lax.dot_general(left, right, (dims, ((), ())), preferred_element_type=F32)


def plane_swap(array, bits):
    return lax.ppermute(array, "ctx", [(i, i ^ bits) for i in range(PLANE)])


def line_turn(array, step):
    return lax.ppermute(array, "wa", [(i, (i + step) % LINE) for i in range(LINE)])


def line_turns(array):
    return [line_turn(array, step) for step in range(1, LINE)]


def relay(from_x, from_y, core):
    passed = jnp.where(core == 0, from_y, from_x)
    pairs = [(i, i ^ 2 if i % 2 == 0 else i ^ 4) for i in range(PLANE)]
    return lax.ppermute(passed, "ctx", pairs)


def pick(array, index):
    return lax.dynamic_index_in_dim(array, index, 0, keepdims=False)


COST = {'cut': 3, 'vectors': 1, 'attend': 12, 'out': 3, 'middle': 17, 'attend_back': 18, 'rest_shard': 4, 'qkv_shard': 2, 'slice_other': 3.0, 'slice_mine': 3.0}
VM = pl.BlockSpec(memory_space=pltpu.VMEM)
SM = pl.BlockSpec(memory_space=pltpu.SMEM)
HB = pl.BlockSpec(memory_space=pl.ANY)
BIG = 56


def call(kernel, inputs, spaces, outputs, scratch=(), mebibytes=32, name=None, own=()):
    shapes = [jax.ShapeDtypeStruct(shape, kind) for shape, kind in outputs]
    return pl.pallas_call(
        kernel,
        out_shape=shapes,
        in_specs=list(spaces),
        out_specs=[HB if i in own else VM for i in range(len(shapes))],
        scratch_shapes=list(scratch),
        compiler_params=pltpu.CompilerParams(vmem_limit_bytes=mebibytes << 20),
        cost_estimate=pl.CostEstimate(flops=int(COST[name] * 1e9), bytes_accessed=1, transcendentals=0),
        name=name,
    )(*inputs)


def place_of(scal):
    return scal[0], scal[1]


def shard_of_turn(line, turn):
    return lax.rem(line - turn + LINE, LINE)


def turn_ahead(line, turn):
    return lax.rem(line + turn, LINE)


def norm_forward(rows):
    middle = jnp.mean(rows, axis=-1, keepdims=True)
    center = rows - middle
    scaled = lax.rsqrt(jnp.mean(center * center, axis=-1, keepdims=True) + NORM_EPS)
    return center * scaled, scaled


def norm_reverse(grad, unit, scaled, gain):
    inner = grad * gain
    return scaled * (
        inner
        - jnp.mean(inner, axis=-1, keepdims=True)
        - unit * jnp.mean(inner * unit, axis=-1, keepdims=True)
    )


def cut_kernel(
    scal, vectors, bias, proj, qkv, up, down, out,
    cols_ref, ups_ref, own_ref,
    qkv_held, up_held, down_held, out_held, sems,
):
    me, line = place_of(scal)
    core = lax.rem(me, 2)
    copies = [
        pltpu.make_async_copy(qkv, qkv_held, sems.at[0]),
        pltpu.make_async_copy(up, up_held, sems.at[1]),
        pltpu.make_async_copy(
            down.at[pl.ds(pl.multiple_of(me * PIECE, 16), PIECE)], down_held, sems.at[2]
        ),
        pltpu.make_async_copy(
            out.at[pl.ds(pl.multiple_of(lax.div(me, 2) * BLOCK, 16), BLOCK)], out_held, sems.at[3]
        ),
    ]
    for copy in copies:
        copy.start()
    rows = [vectors[...].astype(F32)]
    rows += [bias[:, a * SHARD : (a + 1) * SHARD].astype(F32) for a in range(LINE)]
    rows = jnp.concatenate(rows + [jnp.zeros((4, SHARD), F32)])
    own_ref[PARTS + COLS :, :SHARD] = rows.astype(BF16)
    own_ref[PARTS + COLS :, SHARD:] = jnp.zeros((16, SLICE - SHARD), BF16)
    for side in range(2):
        start = FIRST + side * SIDE + PIECE
        for t in range(3):
            own_ref[start : start + 16, t * EMBED : (t + 1) * EMBED] = proj[
                pl.ds(pl.multiple_of(core * HALF + 16 * (3 * side + t), 16), 16), :
            ]
    copies[0].wait()
    for g in range(4):

        @pl.when(lax.rem(me, 4) == g)
        def _():
            for part in range(3):
                start = part * WIDTH + g * WIDE
                cols_ref[:, part * WIDE : (part + 1) * WIDE] = qkv_held[:, start : start + WIDE]

    base = lax.div(me, 4) * HALF
    rows = cols_ref[pl.ds(pl.multiple_of(base, 16), HALF), :]
    own_ref[PARTS : PARTS + HALF, :] = rows[:, :SLICE]
    for side in range(2):
        own_ref[PARTS + HALF : PARTS + COLS, side * WIDE : (side + 1) * WIDE] = rows[
            side * QUARTER : (side + 1) * QUARTER, SLICE:
        ]
    copies[1].wait()
    for k in range(PLANE):
        for s in range(LINE):
            start = s * PLANE * PIECE + k * PIECE
            ups_ref[k, :, s * PIECE : (s + 1) * PIECE] = up_held[:, start : start + PIECE]
    own_ref[:SHARD] = ups_ref[me]
    copies[2].wait()
    for side in range(2):
        start = FIRST + side * SIDE
        own_ref[start : start + PIECE] = down_held[:, side * SLICE : (side + 1) * SLICE]
    copies[3].wait()
    own_ref[SHARD:FIRST] = out_held[:, pl.ds(pl.multiple_of(core * SLICE, 128), SLICE)]


def vectors_kernel(scal, own, halves, full_ref, bias_ref, ends_ref, held):
    me, line = place_of(scal)
    held[line] = own[PARTS + COLS :, :SHARD].astype(F32)
    for turn in range(1, LINE):
        held[shard_of_turn(line, turn)] = halves[turn - 1, COLS:, :SHARD].astype(F32)
    for a in range(LINE):
        full_ref[:, a * SHARD : (a + 1) * SHARD] = held[a, :8, :]
        for k in range(PLANE):
            start = (k % 2) * PIECE
            bias_ref[k : k + 1, a * PIECE : (a + 1) * PIECE] = held[
                a, 8 + k // 2 : 9 + k // 2, start : start + PIECE
            ]
    ends_ref[...] = jnp.zeros((8, PAD), F32)
    ends_ref[:, :WIDE] = held[lax.rem(me, 4), :8, :]


def slots_left(scal, lengths, deal, place):
    me, line = place_of(scal)
    seq = 2 * line + lax.div(me, 4)
    return lengths[seq] - deal[seq, me ^ ORDER[place]] * SPAN


def fill_mask(scal, lengths, deal, mask):
    rows = lax.broadcasted_iota(jnp.int32, (SPAN, SPAN), 0)
    for place in range(PLANE):
        limit = slots_left(scal, lengths, deal, place)
        mask[place * SPAN : (place + 1) * SPAN, :] = jnp.where(rows < limit, 0.0, NEG_FILL)


def head_lanes(h):
    lanes = lax.broadcasted_iota(jnp.int32, (OWN, 128), 1)
    return (lanes >= HEAD) if h % 2 else (lanes < HEAD)


def attend_kernel(
    scal, lengths, deal, ends, own_cols, halves, others, near, far,
    q_out, k_out, v_out, w_out, own_ref, core_ref, x_ref, lse_ref,
    raw, mask, v_turned, o_turned, att, q_ref, k_ref, v_ref, w_ref, sems,
):
    me, line = place_of(scal)
    y = lax.div(me, 4)
    raw[pl.ds(pl.multiple_of(line * SHARD, 16), SHARD), :] = own_cols[...]
    for turn in range(1, LINE):
        base = shard_of_turn(line, turn) * SHARD
        for source, side in ((halves, y), (others, 1 - y)):
            start = base + side * HALF
            at = pl.ds(pl.multiple_of(start, 16), HALF)
            raw[at, :SLICE] = source[turn - 1, :HALF, :]
            for i in range(2):
                at = pl.ds(pl.multiple_of(start + i * QUARTER, 16), QUARTER)
                raw[at, SLICE:] = source[turn - 1, HALF:COLS, i * WIDE : (i + 1) * WIDE]
    fill_mask(scal, lengths, deal, mask)
    for part in range(3):
        w_ref[:, part * PAD : part * PAD + WIDE] = raw[:, part * WIDE : (part + 1) * WIDE]
        w_ref[:, part * PAD + WIDE : (part + 1) * PAD] = jnp.zeros((WIDTH, PAD - WIDE), BF16)
    for t in range(4):
        source = (near, far)[t // 2]
        rows = source[(t % 2) * OWN : (t % 2 + 1) * OWN, :]
        mixed = dot(rows, w_ref[...], NN)
        at = slice(t * OWN, (t + 1) * OWN)
        q_ref[at, :] = ((mixed[:, :PAD] + ends[0:1, :]) * (HEAD ** (-0.5))).astype(BF16)
        k_ref[at, :] = mixed[:, PAD : 2 * PAD].astype(BF16)
        values = mixed[:, 2 * PAD :] + ends[1:2, :]
        v_ref[at, :] = values.astype(BF16)
        v_turned[:, at] = values.T.astype(BF16)

    copies = [
        pltpu.make_async_copy(source, target, sems.at[i])
        for i, (source, target) in enumerate(
            ((q_ref, q_out), (k_ref, k_out), (v_ref, v_out), (w_ref, w_out))
        )
    ]
    for copy in copies:
        copy.start()
    o_turned[WIDE:, :] = jnp.zeros((PAD - WIDE, OWN), F32)

    def tile(t, carry):
        at = pl.ds(pl.multiple_of(t * OWN, OWN), OWN)
        for h in range(HEADS):
            cut = slice((h // 2) * 128, (h // 2 + 1) * 128)
            q_tile = jnp.where(head_lanes(h), q_ref[at, cut], jnp.zeros((), BF16))
            scores = dot(k_ref[:, cut], q_tile, NT)
            scores = scores + jnp.concatenate([mask[...], mask[...]], axis=1)
            peak = jnp.max(scores, axis=0, keepdims=True)
            raised = jnp.exp(scores - peak)
            total = jnp.sum(raised, axis=0, keepdims=True)
            rows = slice(h * HEAD, (h + 1) * HEAD)
            o_turned[rows, :] = dot(v_turned[rows, :], raised.astype(BF16), NN) * (1.0 / total)
            lse_ref[t, h : h + 1, :] = peak + jnp.log(total)
        att[t] = o_turned[...].T.astype(BF16)
        return carry

    lax.fori_loop(0, 4, tile, 0)
    own_ref[...] = att[0]
    core_ref[...] = att[2]
    x_ref[0] = att[1]
    x_ref[1] = att[3]
    for copy in copies:
        copy.wait()


def attend_back_kernel(
    scal, lengths, deal, q_ref, k_ref, v_ref, lse, weights, near, far, first_grad, g0, g1, g2, g3,
    mine_out, other_out, near_out, far_out,
    mine_ref, other_ref, near_ref, far_ref,
    q_held, k_held, v_held, w_held, near_held, far_held, first_held, grads,
    mask, k_turned, q_turned, mixed, key_sum, value_sum, part, sems,
):
    sources = (k_ref, q_ref, v_ref, g0, g1.at[0], g2, g3, weights, near, far, first_grad)
    targets = (k_held, q_held, v_held, grads.at[0], grads.at[1], grads.at[2], grads.at[3])
    targets += (w_held, near_held, far_held, first_held)
    copies = [
        pltpu.make_async_copy(source, target, sems.at[i])
        for i, (source, target) in enumerate(zip(sources, targets, strict=True))
    ]
    for copy in copies:
        copy.start()
    fill_mask(scal, lengths, deal, mask)
    copies[0].wait()
    for t in range(4):
        at = slice(t * OWN, (t + 1) * OWN)
        k_turned[:, at] = k_held[at, :].astype(F32).T.astype(BF16)
    key_sum[...] = jnp.zeros_like(key_sum)
    value_sum[...] = jnp.zeros_like(value_sum)
    q_turned[WIDE:, :] = jnp.zeros((PAD - WIDE, OWN), F32)
    for copy in copies[1:7]:
        copy.wait()

    def tile(t, carry):
        at = pl.ds(pl.multiple_of(t * OWN, OWN), OWN)
        for h in range(HEADS):
            cut = slice((h // 2) * 128, (h // 2 + 1) * 128)
            rows = slice(h * HEAD, (h + 1) * HEAD)
            q_tile = jnp.where(head_lanes(h), q_held[at, cut], jnp.zeros((), BF16))
            g_tile = jnp.where(head_lanes(h), grads[t, :, cut], jnp.zeros((), BF16))
            scores = dot(k_held[:, cut], q_tile, NT)
            scores = scores + jnp.concatenate([mask[...], mask[...]], axis=1)
            probs = jnp.exp(scores - lse[t, h : h + 1, :])
            prob_grad = dot(v_held[:, cut], g_tile, NT)
            delta = jnp.sum(probs * prob_grad, axis=0, keepdims=True)
            score_low = (probs * (prob_grad - delta)).astype(BF16)
            q_turned[rows, :] = dot(k_turned[rows, :], score_low, NN)
            key_sum[:, cut] += dot(score_low, q_tile, NN)
            value_sum[:, cut] += dot(probs.astype(BF16), g_tile, NN)
        low = q_turned[...].T.astype(BF16)
        mixed[at, :PAD] = (low.astype(F32) * (HEAD ** (-0.5))).astype(BF16)
        return carry

    lax.fori_loop(0, 4, tile, 0)
    mixed[:, PAD : 2 * PAD] = key_sum[...].astype(BF16)
    mixed[:, 2 * PAD :] = value_sum[...].astype(BF16)

    me, line = place_of(scal)
    y = lax.div(me, 4)
    for copy in copies[7:]:
        copy.wait()
    for i in range(3):
        cut = slice(i * 256, (i + 1) * 256)
        part[cut, :] = (
            dot(near_held[:, cut], mixed[: 2 * OWN, :], TN) + dot(far_held[:, cut], mixed[2 * OWN :, :], TN)
        ).astype(BF16)
    sums = jnp.sum(mixed[...].astype(F32), axis=0, keepdims=True)
    sums = jnp.concatenate([sums, jnp.zeros((15, 3 * PAD), F32)]).astype(BF16)
    for turn in range(LINE):
        base = turn_ahead(line, turn) * SHARD
        for target, side in ((mine_ref, y), (other_ref, 1 - y)):
            rows = part[pl.ds(pl.multiple_of(base + side * HALF, 16), HALF), :]
            for p in range(3):
                to = slice(p * WIDE, (p + 1) * WIDE)
                target[turn, :HALF, to] = rows[:, p * PAD : p * PAD + WIDE]
                target[turn, HALF:, to] = sums[:, p * PAD : p * PAD + WIDE]
    outs = [
        pltpu.make_async_copy(source, target, sems.at[11 + i])
        for i, (source, target) in enumerate(
            (
                (other_ref, other_out),
                (mine_ref, mine_out),
                (far_ref, far_out),
                (near_ref, near_out),
            )
        )
    ]
    outs[0].start()
    outs[1].start()
    for t in (2, 3, 0, 1):
        at = slice(t * OWN, (t + 1) * OWN)
        token_part = dot(mixed[at, :], w_held[...], NT)
        if t == 0:
            near_ref[at, :] = token_part + first_held[...]
        elif t == 1:
            near_ref[at, :] = token_part
        else:
            far_ref[(t - 2) * OWN : (t - 1) * OWN, :] = token_part.astype(BF16)
        if t == 3:
            outs[2].start()
    outs[3].start()
    for copy in outs:
        copy.wait()


def out_kernel(
    scal, near, full, out_shard, a0, a1, a2, a3, p0, p1, p2, p3, p4, p5, p6, p7,
    sum_ref, low_ref,
    out_ref, sem,
):
    me, line = place_of(scal)
    group = lax.rem(me, 4)
    pieces = (p0, p1, p2, p3, p4, p5, p6, p7)
    copies = []
    for place, bits in enumerate(ORDER):
        k = me ^ bits
        rows = pl.ds(pl.multiple_of(lax.div(k, 2) * BLOCK, 16), BLOCK)
        lanes = pl.ds(pl.multiple_of(lax.rem(k, 2) * SLICE, 128), SLICE)
        for turn in range(1, LINE):
            copies.append(
                pltpu.make_async_copy(
                    pieces[place].at[turn - 1, pl.ds(SHARD, BLOCK)],
                    out_ref.at[shard_of_turn(line, turn), rows, lanes],
                    sem,
                )
            )
    for copy in copies:
        copy.start()
    for z in range(LINE):
        out_ref[z, SHARD:, :] = jnp.zeros((PAD - SHARD, WIDTH), BF16)
    out_ref[line, :SHARD, :] = out_shard[...]
    rows = near[:OWN, :].astype(F32) + full[2:3, :]
    filled = out_ref.at[pl.ds(0, LINE - 1), pl.ds(0, SHARD)]
    pltpu.make_async_copy(filled, filled, sem).wait()
    for i, source in enumerate((a0[...], a1[0], a2[...], a3[...])):
        rows = rows + dot(source, out_ref[group ^ NEAR[i]], NN)
    sum_ref[...] = rows
    unit, _ = norm_forward(rows)
    low_ref[...] = (unit * full[3:4, :] + full[4:5, :]).astype(BF16)


def place_up(scal, place, up_own, held, up_all):
    me, line = place_of(scal)
    at = pl.ds(pl.multiple_of(line * SHARD, 16), SHARD)
    up_all[place, at, :] = up_own[me ^ ORDER[place]]
    for turn in range(1, LINE):
        at = pl.ds(pl.multiple_of(shard_of_turn(line, turn) * SHARD, 16), SHARD)
        up_all[place, at, :] = held[place][turn - 1, :SHARD, :]


def place_down(scal, place, down_own, held, down_all):
    me, line = place_of(scal)
    at = pl.ds(pl.multiple_of(line * PIECE, 16), PIECE)
    start = pl.multiple_of((me ^ ORDER[place]) * PIECE, 16)
    down_all[place, at, :] = down_own[pl.ds(start, PIECE), :]
    for turn in range(1, LINE):
        at = pl.ds(pl.multiple_of(shard_of_turn(line, turn) * PIECE, 16), PIECE)
        for side in range(2):
            start = FIRST + side * SIDE
            down_all[place, at, side * SLICE : (side + 1) * SLICE] = held[place][
                turn - 1, start : start + PIECE, :
            ]


def place_out(scal, place, held, out_all):
    me, line = place_of(scal)
    k = me ^ ORDER[place]
    rows = pl.ds(pl.multiple_of(lax.div(k, 2) * BLOCK, 16), BLOCK)
    lanes = pl.ds(pl.multiple_of(lax.rem(k, 2) * SLICE, 128), SLICE)
    for turn in range(1, LINE):
        out_all[shard_of_turn(line, turn), rows, lanes] = held[place][turn - 1, SHARD:FIRST, :]


def middle_kernel(
    scal, lengths, deal, first_sum, full, bias, proj_shard, out_shard, cot_mine, cot_other, a0, a1, a2, a3, ups, down, p0, p1, p2, p3, p4, p5, p6, p7,
    embed_ref, low_out, first_out, own_out, core_out, x_out, mine_out, other_out,
    low_ref, first_ref, own_ref, core_ref, x_ref, mine_ref, other_ref,
    up_all, down_all, out_all, proj_all, slopes, proj_part, bias_sum, out_part, sems,
):
    held = (p0, p1, p2, p3, p4, p5, p6, p7)
    up_own, down_own = ups, down
    me, line = place_of(scal)
    core, group = lax.rem(me, 2), lax.rem(me, 4)
    proj_all[pl.ds(pl.multiple_of(line * SHARD, 16), SHARD), :] = proj_shard[...]

    unit_one, scale_one = norm_forward(first_sum[...])
    normed = unit_one * full[3:4, :] + full[4:5, :]
    normed_low = normed.astype(BF16)
    second_sum = normed + full[5:6, :]
    for z in range(LINE):
        out_all[z, SHARD:, :] = jnp.zeros((PAD - SHARD, WIDTH), BF16)
    out_all[line, :SHARD, :] = out_shard[...]
    for place, bits in enumerate(ORDER):
        place_up(scal, place, up_own, held, up_all)
        place_down(scal, place, down_own, held, down_all)
        place_out(scal, place, held, out_all)
        inner = dot(normed_low, up_all[place], NN) + bias[pl.ds(me ^ bits, 1), :]
        active, slope = gelu_both(inner)
        slopes[place] = slope
        second_sum = second_sum + dot(active.astype(BF16), down_all[place], NN)
    unit, scaled = norm_forward(second_sum)
    final_low = (unit * full[6:7, :] + full[7:8, :]).astype(BF16)
    for place in (0, 4):
        half = core if place == 0 else 1 - core
        for turn in range(1, LINE):
            base = shard_of_turn(line, turn) * SHARD + half * HALF
            for t in range(6):
                start = FIRST + (t // 3) * SIDE + PIECE
                proj_all[pl.ds(pl.multiple_of(base + 16 * t, 16), 16), :] = held[place][
                    turn - 1, start : start + 16, (t % 3) * EMBED : (t % 3 + 1) * EMBED
                ]
    project = dot(final_low, proj_all[...], NN)
    inverse = lax.rsqrt(jnp.sum(project * project, axis=-1, keepdims=True) + NORM_EPS)
    direction = project * inverse
    rows = lax.broadcasted_iota(jnp.int32, (SPAN, EMBED), 0)
    keep = jnp.concatenate(
        [
            jnp.where(rows < slots_left(scal, lengths, deal, i), 1.0, 0.0).astype(F32)
            for i in range(2)
        ]
    )
    embed_ref[...] = (direction * keep).astype(BF16)
    upstream = jnp.concatenate([cot_mine[...], cot_other[...]]).astype(F32) * keep
    project_grad = (
        inverse * (upstream - direction * jnp.sum(upstream * direction, axis=-1, keepdims=True))
    ).astype(BF16)
    proj_part[...] = dot(final_low, project_grad, TN).astype(BF16)
    final_grad = dot(project_grad, proj_all[...], NT)
    second_grad = norm_reverse(final_grad, unit, scaled, full[6:7, :])
    down_low = second_grad.astype(BF16)
    low_ref[...] = down_low
    outs = [
        pltpu.make_async_copy(source, target, sems.at[i])
        for i, (source, target) in enumerate(
            (
                (low_ref, low_out),
                (x_ref, x_out),
                (core_ref, core_out),
                (own_ref, own_out),
                (first_ref, first_out),
                (other_ref, other_out),
                (mine_ref, mine_out),
            )
        )
    ]
    outs[0].start()

    normed_grad = second_grad
    for place, bits in enumerate(ORDER):
        inner_grad = dot(down_low, down_all[place], NT) * slopes[place]
        bias_sum[pl.ds(me ^ bits, 1), :] = jnp.sum(inner_grad, axis=0, keepdims=True)
        normed_grad = normed_grad + dot(inner_grad.astype(BF16), up_all[place], NT)
    first_grad = norm_reverse(normed_grad, unit_one, scale_one, full[3:4, :])
    first_ref[...] = first_grad
    first_low = first_grad.astype(BF16)
    for i, target in enumerate((own_ref, x_ref.at[0], core_ref, x_ref.at[1])):
        target[...] = dot(first_low, out_all[group ^ NEAR[i]], NT).astype(BF16)
    for copy in outs[1:5]:
        copy.start()
    small = jnp.concatenate(
        [
            jnp.sum(first_grad, axis=0, keepdims=True),
            jnp.sum(normed_grad * unit_one, axis=0, keepdims=True),
            jnp.sum(normed_grad, axis=0, keepdims=True),
            jnp.sum(second_grad, axis=0, keepdims=True),
            jnp.sum(final_grad * unit, axis=0, keepdims=True),
            jnp.sum(final_grad, axis=0, keepdims=True),
            jnp.zeros((2, WIDTH), F32),
        ]
    )
    tail = jnp.concatenate([bias_sum[...], jnp.zeros((8, WIDTH - SLICE), F32)], axis=1)
    small = jnp.concatenate([small, tail]).astype(BF16)
    for i, source in enumerate((a0[...], a1[0], a2[...], a3[...])):
        z = group ^ NEAR[i]
        turn = lax.rem(z - line + LINE, LINE)
        out_part[i] = dot(source, first_low, TN).astype(BF16)
        for target, half in ((mine_ref, core), (other_ref, 1 - core)):
            base = half * HALF
            target[turn, :HALF, :] = out_part[i, pl.ds(pl.multiple_of(base, 16), HALF), :]
            for t in range(6):
                target[turn, HALF : HALF + 16, t * EMBED : (t + 1) * EMBED] = proj_part[
                    pl.ds(pl.multiple_of(z * SHARD + base + 16 * t, 16), 16), :
                ]
            target[turn, HALF + 16 :, :] = small
    outs[5].start()
    outs[6].start()
    for copy in outs:
        copy.wait()


def slice_grad_kernel(
    other, scal, bias, turns, ups, down, n0, n1, n2, n3, d0, d1, d2, d3,
    part_ref,
    held, ups_held, down_held, slots, up_rows, up_turned, down_rows, up_sum, down_sum, up_back,
    sems,
):
    me, line = place_of(scal)
    k = me ^ 1 if other else me
    copies = [
        pltpu.make_async_copy(turns, held, sems.at[0]),
        pltpu.make_async_copy(ups.at[k], ups_held, sems.at[1]),
        pltpu.make_async_copy(
            down.at[pl.ds(pl.multiple_of(k * PIECE, 16), PIECE)], down_held, sems.at[2]
        ),
    ]
    for j, source in enumerate((n0, d0, n1, d1, n2, d2, n3, d3)):
        copies.append(pltpu.make_async_copy(source, slots.at[j], sems.at[3 + j]))
    for copy in copies:
        copy.start()
    for copy in copies[:3]:
        copy.wait()
    for turn in range(LINE):
        z = shard_of_turn(line, turn)
        rows = held[turn - 1, :SHARD, :] if turn else ups_held[...]
        up_rows[pl.ds(pl.multiple_of(z * SHARD, 16), SHARD), :] = rows.astype(F32)
        at = pl.ds(pl.multiple_of(z * PIECE, 16), PIECE)
        if turn == 0:
            down_rows[at, :] = down_held[...]
            continue
        for side in range(2):
            start = FIRST + side * SIDE
            down_rows[at, side * SLICE : (side + 1) * SLICE] = held[
                turn - 1, start : start + PIECE, :
            ]
    up_turned[...] = up_rows[...].T.astype(BF16)
    bias_rows = jnp.broadcast_to(bias[pl.ds(k, 1), :], (128, SLICE)).T
    bias_rows = jnp.concatenate([bias_rows, bias_rows], axis=1)
    for j in range(4):
        copies[3 + 2 * j].wait()
        copies[4 + 2 * j].wait()
        normed, low = slots[2 * j], slots[2 * j + 1]
        inner = dot(up_turned[...], normed, NT) + bias_rows
        active, slope = gelu_both(inner)
        inner_low = (dot(down_rows[...], low, NT) * slope).astype(BF16)
        up_part = dot(inner_low, normed, NN)
        down_part = dot(active.astype(BF16), low, NN)
        if j == 0:
            up_sum[...] = up_part
            down_sum[...] = down_part
        else:
            up_sum[...] += up_part
            down_sum[...] += down_part
    up_back[...] = up_sum[...].T
    for turn in range(LINE):
        z = turn_ahead(line, turn)
        for side in range(2):
            at = pl.ds(pl.multiple_of(z * SHARD + side * HALF, 16), HALF)
            part_ref[turn, :HALF, side * SLICE : (side + 1) * SLICE] = up_back[at, :].astype(BF16)
        at = pl.ds(pl.multiple_of(z * PIECE, 16), PIECE)
        part_ref[turn, HALF:, :] = down_sum[at, :].astype(BF16)


def hold_parts(me, close, far, held):
    for place in range(4):
        held[me ^ ORDER[place]] = close[place][...]
        held[me ^ ORDER[place + 4]] = far[place]


def rest_shard_kernel(
    scal, p0, p1, p2, p3, far,
    up_ref, down_ref, out_ref, proj_ref, rows_ref, bias_ref, held,
):
    me, line = place_of(scal)
    hold_parts(me, (p0, p1, p2, p3), far, held)
    for k in range(PLANE):
        core, x, y = k % 2, (k // 2) % 2, k // 4
        for side in range(2):
            rows = held[k, :HALF, side * SLICE : (side + 1) * SLICE].astype(F32)
            for s in range(LINE):
                start = s * PLANE * PIECE + k * PIECE
                up_ref[side * HALF : (side + 1) * HALF, start : start + PIECE] = rows[
                    :, s * PIECE : (s + 1) * PIECE
                ]
        down_ref[k * PIECE : (k + 1) * PIECE, :] = held[k, HALF : 2 * HALF, :].astype(F32)
        tail = held[k, 2 * HALF :, :].astype(F32)
        block = 2 * x + y
        if block < 3:
            start = core * HALF + 32 * block
            out_ref[start : start + 32, :] = tail
        else:
            for t in range(6):
                start = core * HALF + 16 * t
                proj_ref[start : start + 16, :] = tail[:16, t * EMBED : (t + 1) * EMBED]
            if core == 0:
                small = tail[16:, :]
    for z in range(LINE):

        @pl.when(line == z)
        def _():
            rows_ref[...] = small[:8, z * SHARD : (z + 1) * SHARD]
            bias_ref[...] = small[8:, z * PIECE : (z + 1) * PIECE]


def qkv_shard_kernel(scal, late, p0, p1, p2, p3, far, qkv_ref, rows_ref, held):
    me, line = place_of(scal)
    hold_parts(me, (p0, p1, p2, p3), far, held)
    for k in range(PLANE):
        y, g = k // 4, k % 4
        for part in range(3):
            start = part * WIDTH + g * WIDE
            qkv_ref[y * HALF : (y + 1) * HALF, start : start + WIDE] = held[
                k, :HALF, part * WIDE : (part + 1) * WIDE
            ].astype(F32)
    sums = held[line, HALF:, :].astype(F32)
    rows_ref[...] = jnp.concatenate(
        [sums[:1, :WIDE], sums[:1, 2 * WIDE : 3 * WIDE], late[:6, :]]
    )


def gather_side(array):
    return [array, plane_swap(array, 4), plane_swap(array, 2), plane_swap(array, 6)]


def gather_plane(array):
    close = gather_side(array)
    return close + [plane_swap(jnp.stack(close), 1)]


def turn_parts(parts):
    return [parts[0]] + [line_turn(parts[turn], turn) for turn in range(1, LINE)]


def sum_parts(parts):
    total = parts[0].astype(F32)
    for part in parts[1:]:
        total = total + part.astype(F32)
    return total.astype(BF16)


def swap_groups(own, from_x, for_core):
    return own, from_x, plane_swap(for_core, 1), plane_swap(from_x[1], 1)


def plane_body(
    tokens,
    doc_lengths,
    group_deal,
    qkv_weight,
    out_weight,
    up_weight,
    up_bias,
    down_weight,
    proj_weight,
    vectors,
    cotangent,
):
    me = lax.axis_index("ctx").astype(jnp.int32)
    line = lax.axis_index("wa").astype(jnp.int32)
    y, x, core = me // 4, (me // 2) % 2, me % 2
    scal = jnp.stack([me, line])
    spots = (scal, doc_lengths, group_deal)

    own_cols, ups, own_parts = call(
        cut_kernel,
        (scal, vectors, up_bias.reshape(1, -1), proj_weight)
        + (qkv_weight, up_weight, down_weight, out_weight),
        (SM, VM, VM, VM, HB, HB, HB, HB),
        [
            ((SHARD, 3 * WIDE), BF16),
            ((PLANE, SHARD, SLICE), BF16),
            ((PARTS + COLS + 16, SLICE), BF16),
        ],
        [
            pltpu.VMEM((SHARD, 3 * WIDTH), BF16),
            pltpu.VMEM((SHARD, INNER), BF16),
            pltpu.VMEM((PIECE, WIDTH), BF16),
            pltpu.VMEM((BLOCK, WIDTH), BF16),
            pltpu.SemaphoreType.DMA((4,)),
        ],
        mebibytes=BIG,
        name="cut",
    )
    line_parts = line_turns(own_parts)
    tokens, own_parts = lax.optimization_barrier((tokens, own_parts))
    mine, other = pick(tokens, y), pick(tokens, 1 - y)
    got = [plane_swap(other, 4), plane_swap(mine, 2), plane_swap(other, 6)]
    *line_parts, got_y, got_x, got_d = lax.optimization_barrier((*line_parts, *got))
    near = jnp.concatenate([mine, got_y, got_x, got_d])
    far = plane_swap(near, 1)
    cot_mine, cot_other = pick(cotangent, y), plane_swap(pick(cotangent, 1 - y), 4)
    far, cot_other = lax.optimization_barrier((far, cot_other))
    halves = jnp.stack([part[PARTS:] for part in line_parts])
    others = plane_swap(halves, 4)
    turns = jnp.stack([part[:PARTS] for part in line_parts])
    from_x = plane_swap(turns, 2)
    from_y = plane_swap(turns, 4)

    full, bias, ends = call(
        vectors_kernel,
        (scal, own_parts, halves),
        (SM, VM, VM),
        [((8, WIDTH), F32), ((PLANE, SLICE), F32), ((8, PAD), F32)],
        [pltpu.VMEM((LINE, 16, SHARD), F32)],
        name="vectors",
    )

    queries, keys, values, weights, att_own, att_core, att_x, lse = call(
        attend_kernel,
        (*spots, ends, own_cols, halves, others, near, far),
        (SM, SM, SM, *[VM] * 6),
        [
            ((SLOTS, PAD), BF16),
            ((SLOTS, PAD), BF16),
            ((SLOTS, PAD), BF16),
            ((WIDTH, 3 * PAD), BF16),
            ((OWN, PAD), BF16),
            ((OWN, PAD), BF16),
            ((2, OWN, PAD), BF16),
            ((4, 8, OWN), F32),
        ],
        [
            pltpu.VMEM((WIDTH, 3 * WIDE), BF16),
            pltpu.VMEM((SLOTS, SPAN), F32),
            pltpu.VMEM((PAD, SLOTS), BF16),
            pltpu.VMEM((PAD, OWN), F32),
            pltpu.VMEM((4, OWN, PAD), BF16),
            *[pltpu.VMEM((SLOTS, PAD), BF16)] * 3,
            pltpu.VMEM((WIDTH, 3 * PAD), BF16),
            pltpu.SemaphoreType.DMA((4,)),
        ],
        mebibytes=BIG,
        own=(0, 1, 2, 3),
        name="attend",
    )
    att_x = plane_swap(att_x, 2)
    from_x, from_y, att_x = lax.optimization_barrier((from_x, from_y, att_x))
    from_d = relay(from_x, from_y, core)
    parts = [turns, from_y, from_x, from_d]
    parts += [plane_swap(part, 1) for part in parts]
    groups = swap_groups(att_own, att_x, att_core)

    first_sum, normed_low = call(
        out_kernel,
        (scal, near, full, out_weight, *groups, *parts),
        (SM, VM, VM, VM, *[VM] * 4, *[HB] * 8),
        [
            ((OWN, WIDTH), F32),
            ((OWN, WIDTH), BF16),
        ],
        [pltpu.VMEM((LINE, PAD, WIDTH), BF16), pltpu.SemaphoreType.DMA],
        name="out",
    )
    normed_side = gather_side(normed_low)
    embedded, down_low, first_grad, grad_own, grad_core, grad_x, rest_mine, rest_other = call(
        middle_kernel,
        (*spots, first_sum, full, bias, proj_weight, out_weight, cot_mine, cot_other)
        + (*groups, ups, down_weight, *parts),
        (SM, SM, SM, *[VM] * 21),
        [
            ((OWN, EMBED), BF16),
            ((OWN, WIDTH), BF16),
            ((OWN, WIDTH), F32),
            *[((OWN, PAD), BF16)] * 2,
            ((2, OWN, PAD), BF16),
            *[((LINE, SPAN, WIDTH), BF16)] * 2,
        ],
        [
            pltpu.VMEM((OWN, WIDTH), BF16),
            pltpu.VMEM((OWN, WIDTH), F32),
            *[pltpu.VMEM((OWN, PAD), BF16)] * 2,
            pltpu.VMEM((2, OWN, PAD), BF16),
            *[pltpu.VMEM((LINE, SPAN, WIDTH), BF16)] * 2,
            pltpu.VMEM((PLANE, WIDTH, SLICE), BF16),
            pltpu.VMEM((PLANE, SLICE, WIDTH), BF16),
            pltpu.VMEM((LINE, PAD, WIDTH), BF16),
            pltpu.VMEM((WIDTH, EMBED), BF16),
            pltpu.VMEM((PLANE, OWN, SLICE), F32),
            pltpu.VMEM((WIDTH, EMBED), BF16),
            pltpu.VMEM((PLANE, SLICE), F32),
            pltpu.VMEM((4, PAD, WIDTH), BF16),
            pltpu.SemaphoreType.DMA((7,)),
        ],
        mebibytes=48,
        own=(1, 2, 3, 4, 5, 6, 7),
        name="middle",
    )
    *normed_side, down_low, embedded, grad_core, grad_x, rest_other = lax.optimization_barrier(
        (*normed_side, down_low, embedded, grad_core, grad_x, rest_other)
    )
    down_side = gather_side(down_low)
    embed_other = plane_swap(embedded[SPAN:], 4)
    embeddings = jnp.where(
        y == 0,
        jnp.stack([embedded[:SPAN], embed_other]),
        jnp.stack([embed_other, embedded[:SPAN]]),
    )

    grad_x = plane_swap(grad_x, 2)
    grads = swap_groups(grad_own, grad_x, grad_core)

    rest = rest_mine.astype(F32) + plane_swap(rest_other, 1).astype(F32)
    rest = rest.astype(BF16).reshape(LINE, 2, 64, WIDTH)
    rest_kept = lax.dynamic_index_in_dim(rest, x, 1, keepdims=False)
    rest_sent = lax.dynamic_index_in_dim(rest, 1 - x, 1, keepdims=False)
    rest_sent, first_grad = lax.optimization_barrier((rest_sent, first_grad))
    rest_sent = plane_swap(rest_sent, 2)

    qkv_mine, qkv_other, token_near, token_far = call(
        attend_back_kernel,
        (*spots, queries, keys, values, lse, weights, near, far, first_grad, *grads),
        (SM, SM, SM, HB, HB, HB, VM, *[HB] * 8),
        [
            *[((LINE, HALF + 16, 3 * WIDE), BF16)] * 2,
            ((2 * OWN, WIDTH), F32),
            ((2 * OWN, WIDTH), BF16),
        ],
        [
            *[pltpu.VMEM((LINE, HALF + 16, 3 * WIDE), BF16)] * 2,
            pltpu.VMEM((2 * OWN, WIDTH), F32),
            pltpu.VMEM((2 * OWN, WIDTH), BF16),
            *[pltpu.VMEM((SLOTS, PAD), BF16)] * 3,
            pltpu.VMEM((WIDTH, 3 * PAD), BF16),
            *[pltpu.VMEM((2 * OWN, WIDTH), BF16)] * 2,
            pltpu.VMEM((OWN, WIDTH), F32),
            pltpu.VMEM((4, OWN, PAD), BF16),
            pltpu.VMEM((SLOTS, SPAN), F32),
            pltpu.VMEM((PAD, SLOTS), BF16),
            pltpu.VMEM((PAD, OWN), F32),
            pltpu.VMEM((SLOTS, 3 * PAD), BF16),
            pltpu.VMEM((SLOTS, PAD), F32),
            pltpu.VMEM((SLOTS, PAD), F32),
            pltpu.VMEM((WIDTH, 3 * PAD), BF16),
            pltpu.SemaphoreType.DMA((15,)),
        ],
        mebibytes=BIG,
        own=(0, 1, 2, 3),
        name="attend_back",
    )

    rest = (rest_kept.astype(F32) + rest_sent.astype(F32)).astype(BF16)
    rest = rest.reshape(LINE, 2, 32, WIDTH)
    rest_kept = lax.dynamic_index_in_dim(rest, y, 1, keepdims=False)
    rest_sent = lax.dynamic_index_in_dim(rest, 1 - y, 1, keepdims=False)
    rest_sent = plane_swap(rest_sent, 4)

    *down_side, token_near = lax.optimization_barrier((*down_side, token_near))

    def slice_grad(turns, ups, down, name):
        (parts,) = call(
            partial(slice_grad_kernel, name == "slice_other"),
            (scal, bias, turns, ups, down, *normed_side, *down_side),
            (SM, VM, *[HB] * 11),
            [((LINE, 2 * HALF, WIDTH), BF16)],
            [
                pltpu.VMEM((LINE - 1, PARTS, SLICE), BF16),
                pltpu.VMEM((SHARD, SLICE), BF16),
                pltpu.VMEM((PIECE, WIDTH), BF16),
                pltpu.VMEM((PLANE, OWN, WIDTH), BF16),
                pltpu.VMEM((WIDTH, SLICE), F32),
                *[pltpu.VMEM((SLICE, WIDTH), BF16)] * 2,
                *[pltpu.VMEM((SLICE, WIDTH), F32)] * 2,
                pltpu.VMEM((WIDTH, SLICE), F32),
                pltpu.SemaphoreType.DMA((11,)),
            ],
            mebibytes=BIG,
            name=name,
        )
        return parts

    slices_other = slice_grad(parts[4], ups, down_weight, "slice_other")
    *down_side, slices_other = lax.optimization_barrier((*down_side, slices_other))
    slices_mine = slice_grad(turns, ups, down_weight, "slice_mine")
    slices_other = plane_swap(slices_other, 1)
    slices_mine, rest_sent = lax.optimization_barrier((slices_mine, rest_sent))
    rest = (rest_kept.astype(F32) + rest_sent.astype(F32)).astype(BF16)
    shard_parts = []
    for turn in range(LINE):
        total = slices_mine[turn].astype(F32) + slices_other[turn].astype(F32)
        shard_parts.append(jnp.concatenate([total.astype(BF16), rest[turn]]))
    shard_part = sum_parts(turn_parts(shard_parts))

    qkv_other = plane_swap(qkv_other, 4)
    qkv_parts = [
        (qkv_mine[turn].astype(F32) + qkv_other[turn].astype(F32)).astype(BF16)
        for turn in range(LINE)
    ]
    qkv_part = sum_parts(turn_parts(qkv_parts))

    near_sum = (token_near + plane_swap(token_far, 1).astype(F32)).reshape(4, SPAN, WIDTH)
    pair = near_sum[:2] + plane_swap(near_sum[2:].astype(BF16), 2).astype(F32)
    for_other = plane_swap(pair[1].astype(BF16), 4)
    for_mine, for_other = pair[0], for_other.astype(F32)
    tokens_grad = jnp.where(
        y == 0, jnp.stack([for_mine, for_other]), jnp.stack([for_other, for_mine])
    )
    up_grad, down_grad, out_grad, proj_grad, late_rows, bias_rows = call(
        rest_shard_kernel,
        (scal, *gather_plane(shard_part)),
        (SM, *[VM] * 5),
        [
            ((SHARD, INNER), F32),
            ((WIDTH, WIDTH), F32),
            ((SHARD, WIDTH), F32),
            ((SHARD, EMBED), F32),
            ((8, SHARD), F32),
            ((PLANE, PIECE), F32),
        ],
        [pltpu.VMEM((PLANE, 2 * HALF + 32, WIDTH), BF16)],
        name="rest_shard",
    )
    bias_grad = bias_rows.reshape(-1)
    qkv_grad, vectors_grad = call(
        qkv_shard_kernel,
        (scal, late_rows, *gather_plane(qkv_part)),
        (SM, *[VM] * 6),
        [((SHARD, 3 * WIDTH), F32), ((8, SHARD), F32)],
        [pltpu.VMEM((PLANE, HALF + 16, 3 * WIDE), BF16)],
        name="qkv_shard",
    )
    return (
        embeddings,
        tokens_grad,
        qkv_grad,
        out_grad,
        up_grad,
        bias_grad,
        down_grad,
        proj_grad,
        vectors_grad,
    )


def body(*arrays):
    sequences, span, width = arrays[0].shape
    fits = (
        lax.axis_size("ctx") == PLANE
        and lax.axis_size("wa") == LINE
        and sequences == 2
        and span == SPAN
        and width == WIDTH
    )
    return (plane_body if fits else general_body)(*arrays)


def solution(mesh):
    in_specs = (
        P("wa", "ctx", None),
        P(),
        P(),
        P("wa", None),
        P("wa", None),
        P("wa", None),
        P("wa"),
        P("wa", None),
        P("wa", None),
        P(None, "wa"),
        P("wa", "ctx", None),
    )
    out_specs = (
        P("wa", "ctx", None),
        P("wa", "ctx", None),
        P("wa", None),
        P("wa", None),
        P("wa", None),
        P("wa"),
        P("wa", None),
        P("wa", None),
        P(None, "wa"),
    )
    return jax.shard_map(body, mesh=mesh, in_specs=in_specs, out_specs=out_specs, check_vma=False)
```

profile of v0, /device:TPU:8, one launch (start us, length us, event | category | flops | bytes accessed | tf_op | source)
XLA Modules:
  0.0 263.0 jit_solution(10917268516353852213)
XLA Ops:
  2.5 4.4 %cut.1 = (bf16[192,576]{1,0:T(8,128)(2,1)}, bf16[8,192,384]{2,1,0:T(8,128)(2,1)}, bf16[624,384]{1,0:T(8,128)(2,1)}) custom-call(s32[2]{0:T(128)} %pad_add_fusion.scal, bf16[8,192]{1,0:T(8,128)(2,1)} %vectors.2, bf16[1,768]{1,0:T(2,128)(2,1)} %reshape.73.bias, bf16[192,128]{1,0:T(8,128)(2,1)} %proj_shard.1, bf16[192,2304]{1,0:T(8,128)(2,1)} %qkv.1, ...), custom_call_target="tpu_custom_call" | custom-call | flops 3000000000 | bytes 1 | tf_op jit(solution)/shard_map/cut/pallas_call | solution.py:383
  7.0 3.0 %collective-permute-start.1 = (bf16[624,384]{1,0:T(8,128)(2,1)}, bf16[624,384]{1,0:T(8,128)(2,1)S(1)}, u32[]{:S(2)}, u32[]{:S(2)}) collective-permute-start(bf16[624,384]{1,0:T(8,128)(2,1)} %get-tuple-element.86.own), channel_id=1, source_target_pairs={{0,2},{1,3},{2,0},{3,1},{4,6},{5,7},{6,4},{7,5},{8,10},{9,11},{10,... | collective-permute-start | bytes 1437704 | tf_op jit(solution)/shard_map/ppermute | solution.py:357
  10.0 2.5 collective-permute-start
  15.6 4.9 %collective-permute-done.4 = bf16[128,768]{1,0:T(8,128)(2,1)S(1)} collective-permute-done((bf16[128,768]{1,0:T(8,128)(2,1)S(1)}, bf16[128,768]{1,0:T(8,128)(2,1)S(1)}, u32[]{:S(2)}, u32[]{:S(2)}) %collective-permute-start.4) | collective-permute-done | bytes 196640 | tf_op jit(solution)/shard_map/ppermute | solution.py:353
  24.2 2.8 %collective-permute-done.3 = bf16[128,768]{1,0:T(8,128)(2,1)S(1)} collective-permute-done((bf16[128,768]{1,0:T(8,128)(2,1)S(1)}, bf16[128,768]{1,0:T(8,128)(2,1)S(1)}, u32[]{:S(2)}, u32[]{:S(2)}) %collective-permute-start.3) | collective-permute-done | bytes 196640 | tf_op jit(solution)/shard_map/ppermute | solution.py:353
  27.0 14.6 %collective-permute-done.2 = bf16[624,384]{1,0:T(8,128)(2,1)S(1)} collective-permute-done((bf16[624,384]{1,0:T(8,128)(2,1)}, bf16[624,384]{1,0:T(8,128)(2,1)S(1)}, u32[]{:S(2)}, u32[]{:S(2)}) %collective-permute-start.2) | collective-permute-done | bytes 479264 | tf_op jit(solution)/shard_map/ppermute | solution.py:357
  41.7 9.4 %collective-permute-done = bf16[624,384]{1,0:T(8,128)(2,1)S(1)} collective-permute-done((bf16[624,384]{1,0:T(8,128)(2,1)}, bf16[624,384]{1,0:T(8,128)(2,1)S(1)}, u32[]{:S(2)}, u32[]{:S(2)}) %collective-permute-start) | collective-permute-done | bytes 479264 | tf_op jit(solution)/shard_map/ppermute | solution.py:357
  56.7 6.2 %collective-permute-done.6.others = bf16[3,160,384]{2,1,0:T(8,128)(2,1)S(1)} collective-permute-done((bf16[3,160,384]{2,1,0:T(8,128)(2,1)S(1)}, bf16[3,160,384]{2,1,0:T(8,128)(2,1)S(1)}, u32[]{:S(2)}, u32[]{:S(2)}) %collective-permute-start.6) | collective-permute-done | bytes 368672 | tf_op jit(solution)/shard_map/ppermute | solution.py:353
  63.6 13.5 %attend.1 = (bf16[1024,256]{1,0:T(8,128)(2,1)}, bf16[1024,256]{1,0:T(8,128)(2,1)}, bf16[1024,256]{1,0:T(8,128)(2,1)}, bf16[768,768]{1,0:T(8,128)(2,1)}, bf16[256...) custom-call(s32[2]{0:T(128)} %pad_add_fusion.scal, ...), custom_call_target="tpu_custom_call" | custom-call | flops 12000000000 | bytes 1 | tf_op jit(solution)/shard_map/attend/pallas_call | solution.py:383
  78.7 6.2 %collective-permute-done.11.a1 = bf16[2,256,256]{2,1,0:T(8,128)(2,1)S(1)} collective-permute-done((bf16[2,256,256]{2,1,0:T(8,128)(2,1)}, bf16[2,256,256]{2,1,0:T(8,128)(2,1)S(1)}, u32[]{:S(2)}, u32[]{:S(2)}) %collective-permute-start.11) | collective-permute-done | bytes 262176 | tf_op jit(solution)/shard_map/ppermute | solution.py:353
  87.6 13.0 %collective-permute-done.14.p3 = bf16[3,464,384]{2,1,0:T(8,128)(2,1)S(1)} collective-permute-done((bf16[3,464,384]{2,1,0:T(8,128)(2,1)S(1)}, bf16[3,464,384]{2,1,0:T(8,128)(2,1)S(1)}, u32[]{:S(2)}, u32[]{:S(2)}) %collective-permute-start.14) | collective-permute-done | bytes 1069088 | tf_op jit(solution)/shard_map/ppermute | solution.py:367
  106.9 2.5 collective-permute-start.21
  110.5 17.8 %middle.1 = (bf16[256,128]{1,0:T(8,128)(2,1)S(1)}, bf16[256,768]{1,0:T(8,128)(2,1)S(1)}, f32[256,768]{1,0:T(8,128)S(1)}, bf16[256,256]{1,0:T(8,128)(2,1)S(1)}, b...) custom-call(s32[2]{0:T(128)S(1)} %copy-done.19, ...), custom_call_target="tpu_custom_call" | custom-call | flops 16999999488 | bytes 1 | tf_op jit(solution)/shard_map/middle/pallas_call | solution.py:383
  136.0 4.2 %collective-permute-done.27.g1 = bf16[2,256,256]{2,1,0:T(8,128)(2,1)S(1)} collective-permute-done((bf16[2,256,256]{2,1,0:T(8,128)(2,1)S(1)}, bf16[2,256,256]{2,1,0:T(8,128)(2,1)S(1)}, u32[]{:S(2)}, u32[]{:S(2)}) %collective-permute-start.27) | collective-permute-done | bytes 262176 | tf_op jit(solution)/shard_map/ppermute | solution.py:353
  143.6 19.0 %attend_back.1 = (bf16[4,112,576]{2,1,0:T(8,128)(2,1)}, bf16[4,112,576]{2,1,0:T(8,128)(2,1)}, f32[512,768]{1,0:T(8,128)}, bf16[512,768]{1,0:T(8,128)(2,1)}) custom-call(s32[2]{0:T(128)} %pad_add_fusion.scal, s32[8]{0:T(128)} %lengths.5, s32[8,8]{1,0:T(8,128)} %deal.5, bf16[1024,256]{1,0:T(8,128)(2,1)} %get-tuple-element.112.q_ref, ...), custom_call_target="tpu_custom_call" | custom-call | flops 17999998976 | bytes 1 | tf_op jit(solution)/shard_map/attend_back/pallas_call | solution.py:383
  163.7 7.6 %slice_other.1 = bf16[4,192,768]{2,1,0:T(8,128)(2,1)} custom-call(s32[2]{0:T(128)} %pad_add_fusion.scal, f32[8,384]{1,0:T(8,128)} %copy-done.24, bf16[3,464,384]{2,1,0:T(8,128)(2,1)} %copy-done.6, bf16[8,192,384]{2,1,0:T(8,128)(2,1)} %get-tuple-element.104.ups, bf16[768,768]{1,0:T(8,128)(2,1)} %down.7, bf16[256,768]{1,0:T(8,128)(2,1)} %copy-done.12, ...), custom_call_target="tpu_custom_call" | custom-call | flops 3000000000 | bytes 1 | tf_op jit(solution)/shard_map/slice_other/pallas_call | solution.py:383
  173.1 7.6 %slice_mine.1 = bf16[4,192,768]{2,1,0:T(8,128)(2,1)} custom-call(s32[2]{0:T(128)} %pad_add_fusion.scal, f32[8,384]{1,0:T(8,128)} %copy-done.24, bf16[3,464,384]{2,1,0:T(8,128)(2,1)} %copy-done, bf16[8,192,384]{2,1,0:T(8,128)(2,1)} %get-tuple-element.104.ups, bf16[768,768]{1,0:T(8,128)(2,1)} %down.7, bf16[256,768]{1,0:T(8,128)(2,1)} %copy-done.12, ...), custom_call_target="tpu_custom_call" | custom-call | flops 3000000000 | bytes 1 | tf_op jit(solution)/shard_map/slice_mine/pallas_call | solution.py:383
  183.1 2.4 collective-permute-start.36
  189.0 20.0 %collective-permute-done.36 = bf16[224,768]{1,0:T(8,128)(2,1)S(1)} collective-permute-done((bf16[224,768]{1,0:T(8,128)(2,1)}, bf16[224,768]{1,0:T(8,128)(2,1)S(1)}, u32[]{:S(2)}, u32[]{:S(2)}) %collective-permute-start.36) | collective-permute-done | bytes 344096 | tf_op jit(solution)/shard_map/ppermute | solution.py:357
  208.9 6.6 %collective-permute-done.37 = bf16[224,768]{1,0:T(8,128)(2,1)S(1)} collective-permute-done((bf16[224,768]{1,0:T(8,128)(2,1)}, bf16[224,768]{1,0:T(8,128)(2,1)S(1)}, u32[]{:S(2)}, u32[]{:S(2)}) %collective-permute-start.37) | collective-permute-done | bytes 344096 | tf_op jit(solution)/shard_map/ppermute | solution.py:357
  223.4 5.7 %collective-permute-done.41.p3 = bf16[224,768]{1,0:T(8,128)(2,1)S(1)} collective-permute-done((bf16[224,768]{1,0:T(8,128)(2,1)S(1)}, bf16[224,768]{1,0:T(8,128)(2,1)S(1)}, u32[]{:S(2)}, u32[]{:S(2)}) %collective-permute-start.41) | collective-permute-done | bytes 344096 | tf_op jit(solution)/shard_map/ppermute | solution.py:353
  231.0 3.5 %collective-permute-done.40.p2 = bf16[224,768]{1,0:T(8,128)(2,1)S(1)} collective-permute-done((bf16[224,768]{1,0:T(8,128)(2,1)S(1)}, bf16[224,768]{1,0:T(8,128)(2,1)S(1)}, u32[]{:S(2)}, u32[]{:S(2)}) %collective-permute-start.40) | collective-permute-done | bytes 344096 | tf_op jit(solution)/shard_map/ppermute | solution.py:353
  239.6 7.1 %collective-permute-done.31 = bf16[2,128,768]{2,1,0:T(8,128)(2,1)S(1)} collective-permute-done((bf16[2,128,768]{2,1,0:T(8,128)(2,1)S(1)}, bf16[2,128,768]{2,1,0:T(8,128)(2,1)S(1)}, u32[]{:S(2)}, u32[]{:S(2)}) %collective-permute-start.31) | collective-permute-done | bytes 393248 | tf_op jit(solution)/shard_map/ppermute | solution.py:353
  256.1 3.9 %rest_shard.1 = (f32[192,3072]{1,0:T(8,128)}, f32[768,768]{1,0:T(8,128)}, f32[192,768]{1,0:T(8,128)}, f32[192,128]{1,0:T(8,128)}, f32[8,192]{1,0:T(8,128)S(1)}, /*index=5*/f32[8,96]{1,0:T(8,128)S(1)}) custom-call(s32[2]{0:T(128)S(1)} %copy-done.20, bf16[224,768]{1,0:T(8,128)(2,1)S(1)} %add_convert_fusion.1.p0, ...), custom_call_target="tpu_custom_call" | custom-call | flops 4000000000 | bytes 1 | tf_op jit(solution)/shard_map/rest_shard/pallas_call | solution.py:383
  (218 shorter events, 72.8 us)
Async XLA Ops:
  6.9 34.6 %collective-permute-start.2 = (bf16[624,384]{1,0:T(8,128)(2,1)}, bf16[624,384]{1,0:T(8,128)(2,1)S(1)}, u32[]{:S(2)}, u32[]{:S(2)}) collective-permute-start(bf16[624,384]{1,0:T(8,128)(2,1)} %get-tuple-element.86.own), channel_id=1, source_target_pairs={{0,3},{1,0},{2,1},{3,2},{4,7},{5,4},{6,5},{7,6},{8,11},{9,8},{10,9... | collective-permute-start | bytes 1437704 | tf_op jit(solution)/shard_map/ppermute | solution.py:357
  7.0 34.7 %collective-permute-start.1 = (bf16[624,384]{1,0:T(8,128)(2,1)}, bf16[624,384]{1,0:T(8,128)(2,1)S(1)}, u32[]{:S(2)}, u32[]{:S(2)}) collective-permute-start(bf16[624,384]{1,0:T(8,128)(2,1)} %get-tuple-element.86.own), channel_id=1, source_target_pairs={{0,2},{1,3},{2,0},{3,1},{4,6},{5,7},{6,4},{7,5},{8,10},{9,11},{10,... | collective-permute-start | bytes 1437704 | tf_op jit(solution)/shard_map/ppermute | solution.py:357
  10.0 41.1 %collective-permute-start = (bf16[624,384]{1,0:T(8,128)(2,1)}, bf16[624,384]{1,0:T(8,128)(2,1)S(1)}, u32[]{:S(2)}, u32[]{:S(2)}) collective-permute-start(bf16[624,384]{1,0:T(8,128)(2,1)} %get-tuple-element.86.own), channel_id=1, source_target_pairs={{0,1},{1,2},{2,3},{3,0},{4,5},{5,6},{6,7},{7,4},{8,9},{9,10},{10,1... | collective-permute-start | bytes 1437704 | tf_op jit(solution)/shard_map/ppermute | solution.py:357
  23.7 33.0 %collective-permute-start.8 = (bf16[128,128]{1,0:T(8,128)(2,1)S(1)}, bf16[128,128]{1,0:T(8,128)(2,1)S(1)}, u32[]{:S(2)}, u32[]{:S(2)}) collective-permute-start(bf16[128,128]{1,0:T(8,128)(2,1)S(1)} %get-tuple-element.169), channel_id=1, source_target_pairs={{0,16},{4,20},{8,24},{12,28},{16,0},{20,4},{24,8},{28,12},{1,17},{... | collective-permute-start | bytes 98312 | tf_op jit(solution)/shard_map/ppermute | solution.py:353
  53.3 32.0 %collective-permute-start.10 = (bf16[3,464,384]{2,1,0:T(8,128)(2,1)S(1)}, bf16[3,464,384]{2,1,0:T(8,128)(2,1)S(1)}, u32[]{:S(2)}, u32[]{:S(2)}) collective-permute-start(bf16[3,464,384]{2,1,0:T(8,128)(2,1)S(1)} %pad_maximum_fusion.1.p0.turns), channel_id=1, source_target_pairs={{0,16},{4,20},{8,24},{12,28},{16,0},{20,4},{24,8},{28,12},{1,17},{... | collective-permute-start | bytes 3207176 | tf_op jit(solution)/shard_map/ppermute | solution.py:353
  53.9 31.5 %collective-permute-start.9 = (bf16[3,464,384]{2,1,0:T(8,128)(2,1)S(1)}, bf16[3,464,384]{2,1,0:T(8,128)(2,1)S(1)}, u32[]{:S(2)}, u32[]{:S(2)}) collective-permute-start(bf16[3,464,384]{2,1,0:T(8,128)(2,1)S(1)} %pad_maximum_fusion.1.p0.turns), channel_id=1, source_target_pairs={{0,8},{4,12},{8,0},{12,4},{16,24},{20,28},{24,16},{28,20},{1,9},{5... | collective-permute-start | bytes 3207176 | tf_op jit(solution)/shard_map/ppermute | solution.py:353
  87.1 16.5 %collective-permute-start.15 = (bf16[3,464,384]{2,1,0:T(8,128)(2,1)S(1)}, bf16[3,464,384]{2,1,0:T(8,128)(2,1)S(1)}, u32[]{:S(2)}, u32[]{:S(2)}) collective-permute-start(bf16[3,464,384]{2,1,0:T(8,128)(2,1)S(1)} %pad_maximum_fusion.1.p0.turns), channel_id=1, source_target_pairs={{0,4},{4,0},{8,12},{12,8},{16,20},{20,16},{24,28},{28,24},{1,5},{5... | collective-permute-start | bytes 3207176 | tf_op jit(solution)/shard_map/ppermute | solution.py:353
  87.1 17.8 %collective-permute-start.16 = (bf16[3,464,384]{2,1,0:T(8,128)(2,1)S(1)}, bf16[3,464,384]{2,1,0:T(8,128)(2,1)S(1)}, u32[]{:S(2)}, u32[]{:S(2)}) collective-permute-start(bf16[3,464,384]{2,1,0:T(8,128)(2,1)S(1)} %collective-permute-done.10.p1), channel_id=1, source_target_pairs={{0,4},{4,0},{8,12},{12,8},{16,20},{20,16},{24,28},{28,24},{1,5},{5... | collective-permute-start | bytes 3207176 | tf_op jit(solution)/shard_map/ppermute | solution.py:353
  87.6 17.3 %collective-permute-start.17 = (bf16[3,464,384]{2,1,0:T(8,128)(2,1)S(1)}, bf16[3,464,384]{2,1,0:T(8,128)(2,1)S(1)}, u32[]{:S(2)}, u32[]{:S(2)}) collective-permute-start(bf16[3,464,384]{2,1,0:T(8,128)(2,1)S(1)} %collective-permute-done.9.p2), channel_id=1, source_target_pairs={{0,4},{4,0},{8,12},{12,8},{16,20},{20,16},{24,28},{28,24},{1,5},{5... | collective-permute-start | bytes 3207176 | tf_op jit(solution)/shard_map/ppermute | solution.py:353
  106.9 23.0 %collective-permute-start.21 = (bf16[256,768]{1,0:T(8,128)(2,1)S(1)}, bf16[256,768]{1,0:T(8,128)(2,1)S(1)}, u32[]{:S(2)}, u32[]{:S(2)}) collective-permute-start(bf16[256,768]{1,0:T(8,128)(2,1)S(1)} %get-tuple-element.127.n0), channel_id=1, source_target_pairs={{0,24},{4,28},{8,16},{12,20},{16,8},{20,12},{24,0},{28,4},{1,25},{... | collective-permute-start | bytes 1179656 | tf_op jit(solution)/shard_map/ppermute | solution.py:353
  109.4 20.5 %collective-permute-start.20 = (bf16[256,768]{1,0:T(8,128)(2,1)S(1)}, bf16[256,768]{1,0:T(8,128)(2,1)S(1)}, u32[]{:S(2)}, u32[]{:S(2)}) collective-permute-start(bf16[256,768]{1,0:T(8,128)(2,1)S(1)} %get-tuple-element.127.n0), channel_id=1, source_target_pairs={{0,8},{4,12},{8,0},{12,4},{16,24},{20,28},{24,16},{28,20},{1,9},{5... | collective-permute-start | bytes 1179656 | tf_op jit(solution)/shard_map/ppermute | solution.py:353
  109.9 20.0 %collective-permute-start.19 = (bf16[256,768]{1,0:T(8,128)(2,1)S(1)}, bf16[256,768]{1,0:T(8,128)(2,1)S(1)}, u32[]{:S(2)}, u32[]{:S(2)}) collective-permute-start(bf16[256,768]{1,0:T(8,128)(2,1)S(1)} %get-tuple-element.127.n0), channel_id=1, source_target_pairs={{0,16},{4,20},{8,24},{12,28},{16,0},{20,4},{24,8},{28,12},{1,17},{... | collective-permute-start | bytes 1179656 | tf_op jit(solution)/shard_map/ppermute | solution.py:353
  132.5 30.2 %collective-permute-start.25 = (bf16[256,768]{1,0:T(8,128)(2,1)S(1)}, bf16[256,768]{1,0:T(8,128)(2,1)S(1)}, u32[]{:S(2)}, u32[]{:S(2)}) collective-permute-start(bf16[256,768]{1,0:T(8,128)(2,1)S(1)} %get-tuple-element.135.d0), channel_id=1, source_target_pairs={{0,24},{4,28},{8,16},{12,20},{16,8},{20,12},{24,0},{28,4},{1,25},{... | collective-permute-start | bytes 1179656 | tf_op jit(solution)/shard_map/ppermute | solution.py:353
  134.0 28.7 %collective-permute-start.24 = (bf16[256,768]{1,0:T(8,128)(2,1)S(1)}, bf16[256,768]{1,0:T(8,128)(2,1)S(1)}, u32[]{:S(2)}, u32[]{:S(2)}) collective-permute-start(bf16[256,768]{1,0:T(8,128)(2,1)S(1)} %get-tuple-element.135.d0), channel_id=1, source_target_pairs={{0,8},{4,12},{8,0},{12,4},{16,24},{20,28},{24,16},{28,20},{1,9},{5... | collective-permute-start | bytes 1179656 | tf_op jit(solution)/shard_map/ppermute | solution.py:353
  135.4 27.3 %collective-permute-start.23 = (bf16[256,768]{1,0:T(8,128)(2,1)S(1)}, bf16[256,768]{1,0:T(8,128)(2,1)S(1)}, u32[]{:S(2)}, u32[]{:S(2)}) collective-permute-start(bf16[256,768]{1,0:T(8,128)(2,1)S(1)} %get-tuple-element.135.d0), channel_id=1, source_target_pairs={{0,16},{4,20},{8,24},{12,28},{16,0},{20,4},{24,8},{28,12},{1,17},{... | collective-permute-start | bytes 1179656 | tf_op jit(solution)/shard_map/ppermute | solution.py:353
  141.5 29.9 %collective-permute-start.33 = (bf16[4,64,768]{2,1,0:T(8,128)(2,1)S(1)}, bf16[4,64,768]{2,1,0:T(8,128)(2,1)S(1)}, u32[]{:S(2)}, u32[]{:S(2)}) collective-permute-start(bf16[4,64,768]{2,1,0:T(8,128)(2,1)S(1)} %dynamic-slice_bitcast_fusion), channel_id=1, source_target_pairs={{0,8},{4,12},{8,0},{12,4},{16,24},{20,28},{24,16},{28,20},{1,9},{5... | collective-permute-start | bytes 1179656 | tf_op jit(solution)/shard_map/ppermute | solution.py:353
  183.1 25.9 %collective-permute-start.36 = (bf16[224,768]{1,0:T(8,128)(2,1)}, bf16[224,768]{1,0:T(8,128)(2,1)S(1)}, u32[]{:S(2)}, u32[]{:S(2)}) collective-permute-start(bf16[224,768]{1,0:T(8,128)(2,1)} %pad_maximum_fusion.5), channel_id=1, source_target_pairs={{0,1},{1,2},{2,3},{3,0},{4,5},{5,6},{6,7},{7,4},{8,9},{9,10},{10,1... | collective-permute-start | bytes 1032200 | tf_op jit(solution)/shard_map/ppermute | solution.py:357
  186.2 29.4 %collective-permute-start.37 = (bf16[224,768]{1,0:T(8,128)(2,1)}, bf16[224,768]{1,0:T(8,128)(2,1)S(1)}, u32[]{:S(2)}, u32[]{:S(2)}) collective-permute-start(bf16[224,768]{1,0:T(8,128)(2,1)} %pad_maximum_fusion.6), channel_id=1, source_target_pairs={{0,2},{1,3},{2,0},{3,1},{4,6},{5,7},{6,4},{7,5},{8,10},{9,11},{10,... | collective-permute-start | bytes 1032200 | tf_op jit(solution)/shard_map/ppermute | solution.py:357
  188.0 29.0 %collective-permute-start.38 = (bf16[224,768]{1,0:T(8,128)(2,1)}, bf16[224,768]{1,0:T(8,128)(2,1)S(1)}, u32[]{:S(2)}, u32[]{:S(2)}) collective-permute-start(bf16[224,768]{1,0:T(8,128)(2,1)} %pad_maximum_fusion.7), channel_id=1, source_target_pairs={{0,3},{1,0},{2,1},{3,2},{4,7},{5,4},{6,5},{7,6},{8,11},{9,8},{10,9... | collective-permute-start | bytes 1032200 | tf_op jit(solution)/shard_map/ppermute | solution.py:357
  188.4 32.5 %collective-permute-start.30 = (bf16[512,768]{1,0:T(8,128)(2,1)}, bf16[512,768]{1,0:T(8,128)(2,1)S(1)}, u32[]{:S(2)}, u32[]{:S(2)}) collective-permute-start(bf16[512,768]{1,0:T(8,128)(2,1)} %get-tuple-element.126), channel_id=1, source_target_pairs={{0,4},{4,0},{8,12},{12,8},{16,20},{20,16},{24,28},{28,24},{1,5},{5... | collective-permute-start | bytes 2359304 | tf_op jit(solution)/shard_map/ppermute | solution.py:353
  188.4 32.3 %collective-permute-start.43 = (bf16[4,112,576]{2,1,0:T(8,128)(2,1)}, bf16[4,112,576]{2,1,0:T(8,128)(2,1)S(1)}, u32[]{:S(2)}, u32[]{:S(2)}) collective-permute-start(bf16[4,112,576]{2,1,0:T(8,128)(2,1)} %get-tuple-element.145), channel_id=1, source_target_pairs={{0,16},{4,20},{8,24},{12,28},{16,0},{20,4},{24,8},{28,12},{1,17},{... | collective-permute-start | bytes 1548296 | tf_op jit(solution)/shard_map/ppermute | solution.py:353
  217.7 16.9 %collective-permute-start.40 = (bf16[224,768]{1,0:T(8,128)(2,1)S(1)}, bf16[224,768]{1,0:T(8,128)(2,1)S(1)}, u32[]{:S(2)}, u32[]{:S(2)}) collective-permute-start(bf16[224,768]{1,0:T(8,128)(2,1)S(1)} %add_convert_fusion.1.p0), channel_id=1, source_target_pairs={{0,8},{4,12},{8,0},{12,4},{16,24},{20,28},{24,16},{28,20},{1,9},{5... | collective-permute-start | bytes 1032200 | tf_op jit(solution)/shard_map/ppermute | solution.py:353
  219.2 16.3 %collective-permute-start.39 = (bf16[224,768]{1,0:T(8,128)(2,1)S(1)}, bf16[224,768]{1,0:T(8,128)(2,1)S(1)}, u32[]{:S(2)}, u32[]{:S(2)}) collective-permute-start(bf16[224,768]{1,0:T(8,128)(2,1)S(1)} %add_convert_fusion.1.p0), channel_id=1, source_target_pairs={{0,16},{4,20},{8,24},{12,28},{16,0},{20,4},{24,8},{28,12},{1,17},{... | collective-permute-start | bytes 1032200 | tf_op jit(solution)/shard_map/ppermute | solution.py:353
  235.7 20.4 %collective-permute-start.42 = (bf16[4,224,768]{2,1,0:T(8,128)(2,1)S(1)}, bf16[4,224,768]{2,1,0:T(8,128)(2,1)S(1)}, u32[]{:S(2)}, u32[]{:S(2)}) collective-permute-start(bf16[4,224,768]{2,1,0:T(8,128)(2,1)S(1)} %pad_maximum_fusion), channel_id=1, source_target_pairs={{0,4},{4,0},{8,12},{12,8},{16,20},{20,16},{24,28},{28,24},{1,5},{5... | collective-permute-start | bytes 4128776 | tf_op jit(solution)/shard_map/ppermute | solution.py:353
  (72 other events, 691.2 us)
where the time goes:
time: 267 us; the launch traced here: 263 us
  waiting for transfers between devices  118 us (44%)
  Pallas kernels  78.4 us (29%)
  starting transfers between devices  49.4 us (19%)
  local copies, waits for them, and re-layouts  8.09 us (3%)
  other arithmetic  7.69 us (3%)
    pallas_call x10, Pallas kernels, call(): pl.pallas_call(kernel, out_shape=shapes, in_specs=list(spaces), out_specs...  78.4 us
    ppermute x41, waiting for transfers between devices, plane_swap(): return lax.ppermute(array, 'ctx', [(i, i ^ bits) for i in range(PLANE)])  52.5 us
    ppermute x9, waiting for transfers between devices, line_turn(): lax.ppermute(array, 'wa', [(i, (i + step) % LINE) for i in range(LINE)])  52.2 us
    ppermute x41, starting transfers between devices, plane_swap(): return lax.ppermute(array, 'ctx', [(i, i ^ bits) for i in range(PLANE)])  34.2 us
    ppermute x9, starting transfers between devices, line_turn(): lax.ppermute(array, 'wa', [(i, (i + step) % LINE) for i in range(LINE)])  13.7 us
    ppermute x1, waiting for transfers between devices, relay(): return lax.ppermute(passed, 'ctx', pairs)  13 us
    unnamed x90, local copies, waits for them, and re-layouts  5.71 us
  transfers between devices with their start and end apart: 51, of which 25 were waited for; matrix products, arithmetic and copies ran while one was open for 2% of the time, Pallas kernels for 27%

commit v1 on v0

--- a/solution.py
+++ b/solution.py
@@ -330,7 +330,7 @@
 SLOTS = PLANE * SPAN
 BLOCK = SHARD // 4
 FIRST = SHARD + BLOCK
-SIDE = PIECE + 16
+SIDE = PIECE
 PARTS = FIRST + 2 * SIDE
 QUARTER = HALF // 2
 COLS = HALF + QUARTER
@@ -442,10 +442,10 @@
     rows = [vectors[...].astype(F32)]
     rows += [bias[:, a * SHARD : (a + 1) * SHARD].astype(F32) for a in range(LINE)]
     rows = jnp.concatenate(rows + [jnp.zeros((4, SHARD), F32)])
-    own_ref[PARTS + COLS :, :SHARD] = rows.astype(BF16)
-    own_ref[PARTS + COLS :, SHARD:] = jnp.zeros((16, SLICE - SHARD), BF16)
+    own_ref[PARTS + COLS : PARTS + COLS + 16, :SHARD] = rows.astype(BF16)
+    own_ref[PARTS + COLS : PARTS + COLS + 16, SHARD:] = jnp.zeros((16, SLICE - SHARD), BF16)
     for side in range(2):
-        start = FIRST + side * SIDE + PIECE
+        start = PARTS + COLS + 16 * (1 + side)
         for t in range(3):
             own_ref[start : start + 16, t * EMBED : (t + 1) * EMBED] = proj[
                 pl.ds(pl.multiple_of(core * HALF + 16 * (3 * side + t), 16), 16), :
@@ -482,7 +482,7 @@
 
 def vectors_kernel(scal, own, halves, full_ref, bias_ref, ends_ref, held):
     me, line = place_of(scal)
-    held[line] = own[PARTS + COLS :, :SHARD].astype(F32)
+    held[line] = own[PARTS + COLS : PARTS + COLS + 16, :SHARD].astype(F32)
     for turn in range(1, LINE):
         held[shard_of_turn(line, turn)] = halves[turn - 1, COLS:, :SHARD].astype(F32)
     for a in range(LINE):
@@ -749,7 +749,8 @@
 
 
 def middle_kernel(
-    scal, lengths, deal, first_sum, full, bias, proj_shard, out_shard, cot_mine, cot_other, a0, a1, a2, a3, ups, down, p0, p1, p2, p3, p4, p5, p6, p7,
+    scal, lengths, deal, first_sum, full, bias, proj_shard, out_shard, cot_mine, cot_other,
+    proj_near, proj_far, a0, a1, a2, a3, ups, down, p0, p1, p2, p3, p4, p5, p6, p7,
     embed_ref, low_out, first_out, own_out, core_out, x_out, mine_out, other_out,
     low_ref, first_ref, own_ref, core_ref, x_ref, mine_ref, other_ref,
     up_all, down_all, out_all, proj_all, slopes, proj_part, bias_sum, out_part, sems,
@@ -777,13 +778,12 @@
         second_sum = second_sum + dot(active.astype(BF16), down_all[place], NN)
     unit, scaled = norm_forward(second_sum)
     final_low = (unit * full[6:7, :] + full[7:8, :]).astype(BF16)
-    for place in (0, 4):
-        half = core if place == 0 else 1 - core
+    for half, source in ((core, proj_near), (1 - core, proj_far)):
         for turn in range(1, LINE):
             base = shard_of_turn(line, turn) * SHARD + half * HALF
             for t in range(6):
-                start = FIRST + (t // 3) * SIDE + PIECE
-                proj_all[pl.ds(pl.multiple_of(base + 16 * t, 16), 16), :] = held[place][
+                start = 16 * (t // 3)
+                proj_all[pl.ds(pl.multiple_of(base + 16 * t, 16), 16), :] = source[
                     turn - 1, start : start + 16, (t % 3) * EMBED : (t % 3 + 1) * EMBED
                 ]
     project = dot(final_low, proj_all[...], NN)
@@ -1035,7 +1035,7 @@
         [
             ((SHARD, 3 * WIDE), BF16),
             ((PLANE, SHARD, SLICE), BF16),
-            ((PARTS + COLS + 16, SLICE), BF16),
+            ((PARTS + COLS + 48, SLICE), BF16),
         ],
         [
             pltpu.VMEM((SHARD, 3 * WIDTH), BF16),
@@ -1056,7 +1056,9 @@
     far = plane_swap(near, 1)
     cot_mine, cot_other = pick(cotangent, y), plane_swap(pick(cotangent, 1 - y), 4)
     far, cot_other = lax.optimization_barrier((far, cot_other))
-    halves = jnp.stack([part[PARTS:] for part in line_parts])
+    halves = jnp.stack([part[PARTS : PARTS + COLS + 16] for part in line_parts])
+    proj_near = jnp.stack([part[PARTS + COLS + 16 :] for part in line_parts])
+    proj_far = plane_swap(proj_near, 1)
     others = plane_swap(halves, 4)
     turns = jnp.stack([part[:PARTS] for part in line_parts])
     from_x = plane_swap(turns, 2)
@@ -1102,9 +1104,10 @@
     att_x = plane_swap(att_x, 2)
     from_x, from_y, att_x = lax.optimization_barrier((from_x, from_y, att_x))
     from_d = relay(from_x, from_y, core)
+    groups = list(swap_groups(att_own, att_x, att_core))
+    from_d, groups[2], groups[3] = lax.optimization_barrier((from_d, groups[2], groups[3]))
     parts = [turns, from_y, from_x, from_d]
     parts += [plane_swap(part, 1) for part in parts]
-    groups = swap_groups(att_own, att_x, att_core)
 
     first_sum, normed_low = call(
         out_kernel,
@@ -1121,8 +1124,8 @@
     embedded, down_low, first_grad, grad_own, grad_core, grad_x, rest_mine, rest_other = call(
         middle_kernel,
         (*spots, first_sum, full, bias, proj_weight, out_weight, cot_mine, cot_other)
-        + (*groups, ups, down_weight, *parts),
-        (SM, SM, SM, *[VM] * 21),
+        + (proj_near, proj_far, *groups, ups, down_weight, *parts),
+        (SM, SM, SM, *[VM] * 23),
         [
             ((OWN, EMBED), BF16),
             ((OWN, WIDTH), BF16),

time: 267 us -> 265 us (level)
  waiting for transfers between devices: 118 us -> 110 us
  other arithmetic: 7.69 us -> 10.8 us
    ppermute x41 -> x42, waiting for transfers between devices: 52.5 us -> 47 us  [plane_swap(): return lax.ppermute(array, 'ctx', [(i, i ^ bits) for i in range(PLANE)])]
    ppermute x41 -> x42, starting transfers between devices: 34.2 us -> 34.9 us  [plane_swap(): return lax.ppermute(array, 'ctx', [(i, i ^ bits) for i in range(PLANE)])]
    unnamed x90 -> x88, local copies, waits for them, and re-layouts: 5.71 us -> 5.66 us
  transfers between devices with their start and end apart: 51 -> 52, of which waited for: 25 -> 26; matrix products, arithmetic and copies ran while one was open for 2% -> 4% of each run, Pallas kernels for 27% -> 27%
where the time goes in v1:
time: 265 us; the launch traced here: 261 us
  waiting for transfers between devices  110 us (42%)
  Pallas kernels  78.2 us (30%)
  starting transfers between devices  50.2 us (19%)
  other arithmetic  10.8 us (4%)
  local copies, waits for them, and re-layouts  9.5 us (4%)
    pallas_call x10, Pallas kernels, call(): pl.pallas_call(kernel, out_shape=shapes, in_specs=list(spaces), out_specs...  78.2 us
    ppermute x9, waiting for transfers between devices, line_turn(): lax.ppermute(array, 'wa', [(i, (i + step) % LINE) for i in range(LINE)])  52.2 us
    ppermute x42, waiting for transfers between devices, plane_swap(): return lax.ppermute(array, 'ctx', [(i, i ^ bits) for i in range(PLANE)])  47 us
    ppermute x42, starting transfers between devices, plane_swap(): return lax.ppermute(array, 'ctx', [(i, i ^ bits) for i in range(PLANE)])  34.9 us
    ppermute x9, starting transfers between devices, line_turn(): lax.ppermute(array, 'wa', [(i, (i + step) % LINE) for i in range(LINE)])  13.7 us
    ppermute x1, waiting for transfers between devices, relay(): return lax.ppermute(passed, 'ctx', pairs)  11.2 us
    unnamed x88, local copies, waits for them, and re-layouts  5.66 us
  transfers between devices with their start and end apart: 52, of which 26 were waited for; matrix products, arithmetic and copies ran while one was open for 4% of the time, Pallas kernels for 27%

profile of v1, /device:TPU:8, one launch (start us, length us, event | category | flops | bytes accessed | tf_op | source)
XLA Modules:
  0.0 260.8 jit_solution(7456966298336302610)
XLA Ops:
  2.6 4.4 %cut.1 = (bf16[192,576]{1,0:T(8,128)(2,1)}, bf16[8,192,384]{2,1,0:T(8,128)(2,1)}, bf16[624,384]{1,0:T(8,128)(2,1)}) custom-call(s32[2]{0:T(128)} %pad_add_fusion.scal, bf16[8,192]{1,0:T(8,128)(2,1)} %vectors.2, bf16[1,768]{1,0:T(2,128)(2,1)} %reshape.73.bias, bf16[192,128]{1,0:T(8,128)(2,1)} %proj_shard.1, bf16[192,2304]{1,0:T(8,128)(2,1)} %qkv.1, ...), custom_call_target="tpu_custom_call" | custom-call | flops 3000000000 | bytes 1 | tf_op jit(solution)/shard_map/cut/pallas_call | solution.py:383
  7.1 3.0 %collective-permute-start.1 = (bf16[624,384]{1,0:T(8,128)(2,1)}, bf16[624,384]{1,0:T(8,128)(2,1)S(1)}, u32[]{:S(2)}, u32[]{:S(2)}) collective-permute-start(bf16[624,384]{1,0:T(8,128)(2,1)} %get-tuple-element.89.own), channel_id=1, source_target_pairs={{0,2},{1,3},{2,0},{3,1},{4,6},{5,7},{6,4},{7,5},{8,10},{9,11},{10,... | collective-permute-start | bytes 1437704 | tf_op jit(solution)/shard_map/ppermute | solution.py:357
  10.1 2.5 collective-permute-start
  15.6 4.9 %collective-permute-done.4 = bf16[128,768]{1,0:T(8,128)(2,1)S(1)} collective-permute-done((bf16[128,768]{1,0:T(8,128)(2,1)S(1)}, bf16[128,768]{1,0:T(8,128)(2,1)S(1)}, u32[]{:S(2)}, u32[]{:S(2)}) %collective-permute-start.4) | collective-permute-done | bytes 196640 | tf_op jit(solution)/shard_map/ppermute | solution.py:353
  24.2 2.8 %collective-permute-done.3 = bf16[128,768]{1,0:T(8,128)(2,1)S(1)} collective-permute-done((bf16[128,768]{1,0:T(8,128)(2,1)S(1)}, bf16[128,768]{1,0:T(8,128)(2,1)S(1)}, u32[]{:S(2)}, u32[]{:S(2)}) %collective-permute-start.3) | collective-permute-done | bytes 196640 | tf_op jit(solution)/shard_map/ppermute | solution.py:353
  27.0 14.6 %collective-permute-done.2 = bf16[624,384]{1,0:T(8,128)(2,1)S(1)} collective-permute-done((bf16[624,384]{1,0:T(8,128)(2,1)}, bf16[624,384]{1,0:T(8,128)(2,1)S(1)}, u32[]{:S(2)}, u32[]{:S(2)}) %collective-permute-start.2) | collective-permute-done | bytes 479264 | tf_op jit(solution)/shard_map/ppermute | solution.py:357
  41.8 9.4 %collective-permute-done = bf16[624,384]{1,0:T(8,128)(2,1)S(1)} collective-permute-done((bf16[624,384]{1,0:T(8,128)(2,1)}, bf16[624,384]{1,0:T(8,128)(2,1)S(1)}, u32[]{:S(2)}, u32[]{:S(2)}) %collective-permute-start) | collective-permute-done | bytes 479264 | tf_op jit(solution)/shard_map/ppermute | solution.py:357
  56.8 6.2 %collective-permute-done.6.others = bf16[3,160,384]{2,1,0:T(8,128)(2,1)S(1)} collective-permute-done((bf16[3,160,384]{2,1,0:T(8,128)(2,1)S(1)}, bf16[3,160,384]{2,1,0:T(8,128)(2,1)S(1)}, u32[]{:S(2)}, u32[]{:S(2)}) %collective-permute-start.6) | collective-permute-done | bytes 368672 | tf_op jit(solution)/shard_map/ppermute | solution.py:353
  63.7 13.5 %attend.1 = (bf16[1024,256]{1,0:T(8,128)(2,1)}, bf16[1024,256]{1,0:T(8,128)(2,1)}, bf16[1024,256]{1,0:T(8,128)(2,1)}, bf16[768,768]{1,0:T(8,128)(2,1)}, bf16[256...) custom-call(s32[2]{0:T(128)} %pad_add_fusion.scal, ...), custom_call_target="tpu_custom_call" | custom-call | flops 12000000000 | bytes 1 | tf_op jit(solution)/shard_map/attend/pallas_call | solution.py:383
  78.8 5.1 %collective-permute-done.10.p1 = bf16[3,432,384]{2,1,0:T(8,128)(2,1)S(1)} collective-permute-done((bf16[3,432,384]{2,1,0:T(8,128)(2,1)S(1)}, bf16[3,432,384]{2,1,0:T(8,128)(2,1)S(1)}, u32[]{:S(2)}, u32[]{:S(2)}) %collective-permute-start.10) | collective-permute-done | bytes 995360 | tf_op jit(solution)/shard_map/ppermute | solution.py:353
  88.3 11.2 %collective-permute-done.12.p3 = bf16[3,432,384]{2,1,0:T(8,128)(2,1)S(1)} collective-permute-done((bf16[3,432,384]{2,1,0:T(8,128)(2,1)S(1)}, bf16[3,432,384]{2,1,0:T(8,128)(2,1)S(1)}, u32[]{:S(2)}, u32[]{:S(2)}) %collective-permute-start.12) | collective-permute-done | bytes 995360 | tf_op jit(solution)/shard_map/ppermute | solution.py:367
  104.0 2.5 collective-permute-start.21
  107.5 17.7 %middle.1 = (bf16[256,128]{1,0:T(8,128)(2,1)S(1)}, bf16[256,768]{1,0:T(8,128)(2,1)S(1)}, f32[256,768]{1,0:T(8,128)S(1)}, bf16[256,256]{1,0:T(8,128)(2,1)S(1)}, b...) custom-call(s32[2]{0:T(128)S(1)} %copy-done.19, ...), custom_call_target="tpu_custom_call" | custom-call | flops 16999999488 | bytes 1 | tf_op jit(solution)/shard_map/middle/pallas_call | solution.py:383
  132.9 4.2 %collective-permute-done.28.g1 = bf16[2,256,256]{2,1,0:T(8,128)(2,1)S(1)} collective-permute-done((bf16[2,256,256]{2,1,0:T(8,128)(2,1)S(1)}, bf16[2,256,256]{2,1,0:T(8,128)(2,1)S(1)}, u32[]{:S(2)}, u32[]{:S(2)}) %collective-permute-start.28) | collective-permute-done | bytes 262176 | tf_op jit(solution)/shard_map/ppermute | solution.py:353
  140.5 19.0 %attend_back.1 = (bf16[4,112,576]{2,1,0:T(8,128)(2,1)}, bf16[4,112,576]{2,1,0:T(8,128)(2,1)}, f32[512,768]{1,0:T(8,128)}, bf16[512,768]{1,0:T(8,128)(2,1)}) custom-call(s32[2]{0:T(128)} %pad_add_fusion.scal, s32[8]{0:T(128)} %lengths.5, s32[8,8]{1,0:T(8,128)} %deal.5, bf16[1024,256]{1,0:T(8,128)(2,1)} %get-tuple-element.118.q_ref, ...), custom_call_target="tpu_custom_call" | custom-call | flops 17999998976 | bytes 1 | tf_op jit(solution)/shard_map/attend_back/pallas_call | solution.py:383
  160.6 7.5 %slice_other.1 = bf16[4,192,768]{2,1,0:T(8,128)(2,1)} custom-call(s32[2]{0:T(128)} %pad_add_fusion.scal, f32[8,384]{1,0:T(8,128)} %copy-done.22, bf16[3,432,384]{2,1,0:T(8,128)(2,1)} %copy-done.6, bf16[8,192,384]{2,1,0:T(8,128)(2,1)} %get-tuple-element.110.ups, bf16[768,768]{1,0:T(8,128)(2,1)} %down.7, bf16[256,768]{1,0:T(8,128)(2,1)} %copy-done.12, ...), custom_call_target="tpu_custom_call" | custom-call | flops 3000000000 | bytes 1 | tf_op jit(solution)/shard_map/slice_other/pallas_call | solution.py:383
  170.0 7.6 %slice_mine.1 = bf16[4,192,768]{2,1,0:T(8,128)(2,1)} custom-call(s32[2]{0:T(128)} %pad_add_fusion.scal, f32[8,384]{1,0:T(8,128)} %copy-done.22, bf16[3,432,384]{2,1,0:T(8,128)(2,1)} %copy-done, bf16[8,192,384]{2,1,0:T(8,128)(2,1)} %get-tuple-element.110.ups, bf16[768,768]{1,0:T(8,128)(2,1)} %down.7, bf16[256,768]{1,0:T(8,128)(2,1)} %copy-done.12, ...), custom_call_target="tpu_custom_call" | custom-call | flops 3000000000 | bytes 1 | tf_op jit(solution)/shard_map/slice_mine/pallas_call | solution.py:383
  179.9 2.4 collective-permute-start.37
  185.8 20.0 %collective-permute-done.37 = bf16[224,768]{1,0:T(8,128)(2,1)S(1)} collective-permute-done((bf16[224,768]{1,0:T(8,128)(2,1)}, bf16[224,768]{1,0:T(8,128)(2,1)S(1)}, u32[]{:S(2)}, u32[]{:S(2)}) %collective-permute-start.37) | collective-permute-done | bytes 344096 | tf_op jit(solution)/shard_map/ppermute | solution.py:357
  205.8 6.6 %collective-permute-done.38 = bf16[224,768]{1,0:T(8,128)(2,1)} collective-permute-done((bf16[224,768]{1,0:T(8,128)(2,1)}, bf16[224,768]{1,0:T(8,128)(2,1)}, u32[]{:S(2)}, u32[]{:S(2)}) %collective-permute-start.38) | collective-permute-done | bytes 344096 | tf_op jit(solution)/shard_map/ppermute | solution.py:357
  222.4 4.5 %collective-permute-done.42.p3 = bf16[224,768]{1,0:T(8,128)(2,1)S(1)} collective-permute-done((bf16[224,768]{1,0:T(8,128)(2,1)S(1)}, bf16[224,768]{1,0:T(8,128)(2,1)S(1)}, u32[]{:S(2)}, u32[]{:S(2)}) %collective-permute-start.42) | collective-permute-done | bytes 344096 | tf_op jit(solution)/shard_map/ppermute | solution.py:353
  228.9 3.4 %collective-permute-done.41.p2 = bf16[224,768]{1,0:T(8,128)(2,1)S(1)} collective-permute-done((bf16[224,768]{1,0:T(8,128)(2,1)S(1)}, bf16[224,768]{1,0:T(8,128)(2,1)S(1)}, u32[]{:S(2)}, u32[]{:S(2)}) %collective-permute-start.41) | collective-permute-done | bytes 344096 | tf_op jit(solution)/shard_map/ppermute | solution.py:353
  238.3 6.1 %collective-permute-done.32 = bf16[2,128,768]{2,1,0:T(8,128)(2,1)S(1)} collective-permute-done((bf16[2,128,768]{2,1,0:T(8,128)(2,1)S(1)}, bf16[2,128,768]{2,1,0:T(8,128)(2,1)S(1)}, u32[]{:S(2)}, u32[]{:S(2)}) %collective-permute-start.32) | collective-permute-done | bytes 393248 | tf_op jit(solution)/shard_map/ppermute | solution.py:353
  253.9 3.9 %rest_shard.1 = (f32[192,3072]{1,0:T(8,128)}, f32[768,768]{1,0:T(8,128)}, f32[192,768]{1,0:T(8,128)}, f32[192,128]{1,0:T(8,128)}, f32[8,192]{1,0:T(8,128)S(1)}, /*index=5*/f32[8,96]{1,0:T(8,128)S(1)}) custom-call(s32[2]{0:T(128)S(1)} %copy-done.20, bf16[224,768]{1,0:T(8,128)(2,1)S(1)} %add_convert_fusion.1.p0, ...), custom_call_target="tpu_custom_call" | custom-call | flops 4000000000 | bytes 1 | tf_op jit(solution)/shard_map/rest_shard/pallas_call | solution.py:383
  (221 shorter events, 76.1 us)
Async XLA Ops:
  7.0 34.6 %collective-permute-start.2 = (bf16[624,384]{1,0:T(8,128)(2,1)}, bf16[624,384]{1,0:T(8,128)(2,1)S(1)}, u32[]{:S(2)}, u32[]{:S(2)}) collective-permute-start(bf16[624,384]{1,0:T(8,128)(2,1)} %get-tuple-element.89.own), channel_id=1, source_target_pairs={{0,3},{1,0},{2,1},{3,2},{4,7},{5,4},{6,5},{7,6},{8,11},{9,8},{10,9... | collective-permute-start | bytes 1437704 | tf_op jit(solution)/shard_map/ppermute | solution.py:357
  7.1 34.7 %collective-permute-start.1 = (bf16[624,384]{1,0:T(8,128)(2,1)}, bf16[624,384]{1,0:T(8,128)(2,1)S(1)}, u32[]{:S(2)}, u32[]{:S(2)}) collective-permute-start(bf16[624,384]{1,0:T(8,128)(2,1)} %get-tuple-element.89.own), channel_id=1, source_target_pairs={{0,2},{1,3},{2,0},{3,1},{4,6},{5,7},{6,4},{7,5},{8,10},{9,11},{10,... | collective-permute-start | bytes 1437704 | tf_op jit(solution)/shard_map/ppermute | solution.py:357
  10.1 41.1 %collective-permute-start = (bf16[624,384]{1,0:T(8,128)(2,1)}, bf16[624,384]{1,0:T(8,128)(2,1)S(1)}, u32[]{:S(2)}, u32[]{:S(2)}) collective-permute-start(bf16[624,384]{1,0:T(8,128)(2,1)} %get-tuple-element.89.own), channel_id=1, source_target_pairs={{0,1},{1,2},{2,3},{3,0},{4,5},{5,6},{6,7},{7,4},{8,9},{9,10},{10,1... | collective-permute-start | bytes 1437704 | tf_op jit(solution)/shard_map/ppermute | solution.py:357
  23.7 33.0 %collective-permute-start.8 = (bf16[128,128]{1,0:T(8,128)(2,1)S(1)}, bf16[128,128]{1,0:T(8,128)(2,1)S(1)}, u32[]{:S(2)}, u32[]{:S(2)}) collective-permute-start(bf16[128,128]{1,0:T(8,128)(2,1)S(1)} %get-tuple-element.175), channel_id=1, source_target_pairs={{0,16},{4,20},{8,24},{12,28},{16,0},{20,4},{24,8},{28,12},{1,17},{... | collective-permute-start | bytes 98312 | tf_op jit(solution)/shard_map/ppermute | solution.py:353
  53.4 30.5 %collective-permute-start.10 = (bf16[3,432,384]{2,1,0:T(8,128)(2,1)S(1)}, bf16[3,432,384]{2,1,0:T(8,128)(2,1)S(1)}, u32[]{:S(2)}, u32[]{:S(2)}) collective-permute-start(bf16[3,432,384]{2,1,0:T(8,128)(2,1)S(1)} %pad_maximum_fusion.1.p0.turns), channel_id=1, source_target_pairs={{0,16},{4,20},{8,24},{12,28},{16,0},{20,4},{24,8},{28,12},{1,17},{... | collective-permute-start | bytes 2985992 | tf_op jit(solution)/shard_map/ppermute | solution.py:353
  54.0 29.9 %collective-permute-start.9 = (bf16[3,432,384]{2,1,0:T(8,128)(2,1)S(1)}, bf16[3,432,384]{2,1,0:T(8,128)(2,1)S(1)}, u32[]{:S(2)}, u32[]{:S(2)}) collective-permute-start(bf16[3,432,384]{2,1,0:T(8,128)(2,1)S(1)} %pad_maximum_fusion.1.p0.turns), channel_id=1, source_target_pairs={{0,8},{4,12},{8,0},{12,4},{16,24},{20,28},{24,16},{28,20},{1,9},{5... | collective-permute-start | bytes 2985992 | tf_op jit(solution)/shard_map/ppermute | solution.py:353
  85.1 14.3 %collective-permute-start.12 = (bf16[3,432,384]{2,1,0:T(8,128)(2,1)S(1)}, bf16[3,432,384]{2,1,0:T(8,128)(2,1)S(1)}, u32[]{:S(2)}, u32[]{:S(2)}) collective-permute-start(bf16[3,432,384]{2,1,0:T(8,128)(2,1)S(1)} %broadcast_select_fusion), channel_id=1, source_target_pairs={{0,8},{4,20},{8,0},{12,28},{16,24},{20,4},{24,16},{28,12},{1,9},{5... | collective-permute-start | bytes 2985992 | tf_op jit(solution)/shard_map/ppermute | solution.py:367
  87.3 14.2 %collective-permute-start.15 = (bf16[3,432,384]{2,1,0:T(8,128)(2,1)S(1)}, bf16[3,432,384]{2,1,0:T(8,128)(2,1)S(1)}, u32[]{:S(2)}, u32[]{:S(2)}) collective-permute-start(bf16[3,432,384]{2,1,0:T(8,128)(2,1)S(1)} %pad_maximum_fusion.1.p0.turns), channel_id=1, source_target_pairs={{0,4},{4,0},{8,12},{12,8},{16,20},{20,16},{24,28},{28,24},{1,5},{5... | collective-permute-start | bytes 2985992 | tf_op jit(solution)/shard_map/ppermute | solution.py:353
  104.0 22.8 %collective-permute-start.21 = (bf16[256,768]{1,0:T(8,128)(2,1)S(1)}, bf16[256,768]{1,0:T(8,128)(2,1)S(1)}, u32[]{:S(2)}, u32[]{:S(2)}) collective-permute-start(bf16[256,768]{1,0:T(8,128)(2,1)S(1)} %get-tuple-element.133.n0), channel_id=1, source_target_pairs={{0,24},{4,28},{8,16},{12,20},{16,8},{20,12},{24,0},{28,4},{1,25},{... | collective-permute-start | bytes 1179656 | tf_op jit(solution)/shard_map/ppermute | solution.py:353
  106.5 20.3 %collective-permute-start.20 = (bf16[256,768]{1,0:T(8,128)(2,1)S(1)}, bf16[256,768]{1,0:T(8,128)(2,1)S(1)}, u32[]{:S(2)}, u32[]{:S(2)}) collective-permute-start(bf16[256,768]{1,0:T(8,128)(2,1)S(1)} %get-tuple-element.133.n0), channel_id=1, source_target_pairs={{0,8},{4,12},{8,0},{12,4},{16,24},{20,28},{24,16},{28,20},{1,9},{5... | collective-permute-start | bytes 1179656 | tf_op jit(solution)/shard_map/ppermute | solution.py:353
  107.0 19.8 %collective-permute-start.19 = (bf16[256,768]{1,0:T(8,128)(2,1)S(1)}, bf16[256,768]{1,0:T(8,128)(2,1)S(1)}, u32[]{:S(2)}, u32[]{:S(2)}) collective-permute-start(bf16[256,768]{1,0:T(8,128)(2,1)S(1)} %get-tuple-element.133.n0), channel_id=1, source_target_pairs={{0,16},{4,20},{8,24},{12,28},{16,0},{20,4},{24,8},{28,12},{1,17},{... | collective-permute-start | bytes 1179656 | tf_op jit(solution)/shard_map/ppermute | solution.py:353
  129.4 30.2 %collective-permute-start.26 = (bf16[256,768]{1,0:T(8,128)(2,1)S(1)}, bf16[256,768]{1,0:T(8,128)(2,1)S(1)}, u32[]{:S(2)}, u32[]{:S(2)}) collective-permute-start(bf16[256,768]{1,0:T(8,128)(2,1)S(1)} %get-tuple-element.141.d0), channel_id=1, source_target_pairs={{0,24},{4,28},{8,16},{12,20},{16,8},{20,12},{24,0},{28,4},{1,25},{... | collective-permute-start | bytes 1179656 | tf_op jit(solution)/shard_map/ppermute | solution.py:353
  130.9 28.7 %collective-permute-start.25 = (bf16[256,768]{1,0:T(8,128)(2,1)S(1)}, bf16[256,768]{1,0:T(8,128)(2,1)S(1)}, u32[]{:S(2)}, u32[]{:S(2)}) collective-permute-start(bf16[256,768]{1,0:T(8,128)(2,1)S(1)} %get-tuple-element.141.d0), channel_id=1, source_target_pairs={{0,8},{4,12},{8,0},{12,4},{16,24},{20,28},{24,16},{28,20},{1,9},{5... | collective-permute-start | bytes 1179656 | tf_op jit(solution)/shard_map/ppermute | solution.py:353
  132.4 27.3 %collective-permute-start.24 = (bf16[256,768]{1,0:T(8,128)(2,1)S(1)}, bf16[256,768]{1,0:T(8,128)(2,1)S(1)}, u32[]{:S(2)}, u32[]{:S(2)}) collective-permute-start(bf16[256,768]{1,0:T(8,128)(2,1)S(1)} %get-tuple-element.141.d0), channel_id=1, source_target_pairs={{0,16},{4,20},{8,24},{12,28},{16,0},{20,4},{24,8},{28,12},{1,17},{... | collective-permute-start | bytes 1179656 | tf_op jit(solution)/shard_map/ppermute | solution.py:353
  138.4 29.9 %collective-permute-start.34 = (bf16[4,64,768]{2,1,0:T(8,128)(2,1)S(1)}, bf16[4,64,768]{2,1,0:T(8,128)(2,1)S(1)}, u32[]{:S(2)}, u32[]{:S(2)}) collective-permute-start(bf16[4,64,768]{2,1,0:T(8,128)(2,1)S(1)} %dynamic-slice_bitcast_fusion), channel_id=1, source_target_pairs={{0,8},{4,12},{8,0},{12,4},{16,24},{20,28},{24,16},{28,20},{1,9},{5... | collective-permute-start | bytes 1179656 | tf_op jit(solution)/shard_map/ppermute | solution.py:353
  179.9 25.9 %collective-permute-start.37 = (bf16[224,768]{1,0:T(8,128)(2,1)}, bf16[224,768]{1,0:T(8,128)(2,1)S(1)}, u32[]{:S(2)}, u32[]{:S(2)}) collective-permute-start(bf16[224,768]{1,0:T(8,128)(2,1)} %pad_maximum_fusion.5), channel_id=1, source_target_pairs={{0,1},{1,2},{2,3},{3,0},{4,5},{5,6},{6,7},{7,4},{8,9},{9,10},{10,1... | collective-permute-start | bytes 1032200 | tf_op jit(solution)/shard_map/ppermute | solution.py:357
  183.0 29.4 %collective-permute-start.38 = (bf16[224,768]{1,0:T(8,128)(2,1)}, bf16[224,768]{1,0:T(8,128)(2,1)}, u32[]{:S(2)}, u32[]{:S(2)}) collective-permute-start(bf16[224,768]{1,0:T(8,128)(2,1)} %pad_maximum_fusion.6), channel_id=1, source_target_pairs={{0,2},{1,3},{2,0},{3,1},{4,6},{5,7},{6,4},{7,5},{8,10},{9,11},{10,... | collective-permute-start | bytes 1032200 | tf_op jit(solution)/shard_map/ppermute | solution.py:357
  184.8 29.0 %collective-permute-start.39 = (bf16[224,768]{1,0:T(8,128)(2,1)}, bf16[224,768]{1,0:T(8,128)(2,1)S(1)}, u32[]{:S(2)}, u32[]{:S(2)}) collective-permute-start(bf16[224,768]{1,0:T(8,128)(2,1)} %pad_maximum_fusion.7), channel_id=1, source_target_pairs={{0,3},{1,0},{2,1},{3,2},{4,7},{5,4},{6,5},{7,6},{8,11},{9,8},{10,9... | collective-permute-start | bytes 1032200 | tf_op jit(solution)/shard_map/ppermute | solution.py:357
  185.2 34.7 %collective-permute-start.31 = (bf16[512,768]{1,0:T(8,128)(2,1)}, bf16[512,768]{1,0:T(8,128)(2,1)S(1)}, u32[]{:S(2)}, u32[]{:S(2)}) collective-permute-start(bf16[512,768]{1,0:T(8,128)(2,1)} %get-tuple-element.132), channel_id=1, source_target_pairs={{0,4},{4,0},{8,12},{12,8},{16,20},{20,16},{24,28},{28,24},{1,5},{5... | collective-permute-start | bytes 2359304 | tf_op jit(solution)/shard_map/ppermute | solution.py:353
  185.2 33.3 %collective-permute-start.44 = (bf16[4,112,576]{2,1,0:T(8,128)(2,1)}, bf16[4,112,576]{2,1,0:T(8,128)(2,1)}, u32[]{:S(2)}, u32[]{:S(2)}) collective-permute-start(bf16[4,112,576]{2,1,0:T(8,128)(2,1)} %get-tuple-element.151), channel_id=1, source_target_pairs={{0,16},{4,20},{8,24},{12,28},{16,0},{20,4},{24,8},{28,12},{1,17},{... | collective-permute-start | bytes 1548296 | tf_op jit(solution)/shard_map/ppermute | solution.py:353
  215.5 16.9 %collective-permute-start.41 = (bf16[224,768]{1,0:T(8,128)(2,1)S(1)}, bf16[224,768]{1,0:T(8,128)(2,1)S(1)}, u32[]{:S(2)}, u32[]{:S(2)}) collective-permute-start(bf16[224,768]{1,0:T(8,128)(2,1)S(1)} %add_convert_fusion.1.p0), channel_id=1, source_target_pairs={{0,8},{4,12},{8,0},{12,4},{16,24},{20,28},{24,16},{28,20},{1,9},{5... | collective-permute-start | bytes 1032200 | tf_op jit(solution)/shard_map/ppermute | solution.py:353
  217.0 16.3 %collective-permute-start.40 = (bf16[224,768]{1,0:T(8,128)(2,1)S(1)}, bf16[224,768]{1,0:T(8,128)(2,1)S(1)}, u32[]{:S(2)}, u32[]{:S(2)}) collective-permute-start(bf16[224,768]{1,0:T(8,128)(2,1)S(1)} %add_convert_fusion.1.p0), channel_id=1, source_target_pairs={{0,16},{4,20},{8,24},{12,28},{16,0},{20,4},{24,8},{28,12},{1,17},{... | collective-permute-start | bytes 1032200 | tf_op jit(solution)/shard_map/ppermute | solution.py:353
  219.9 14.8 %collective-permute-start.47 = (bf16[112,576]{1,0:T(8,128)(2,1)S(1)}, bf16[112,576]{1,0:T(8,128)(2,1)S(1)}, u32[]{:S(2)}, u32[]{:S(2)}) collective-permute-start(bf16[112,576]{1,0:T(8,128)(2,1)S(1)} %get-tuple-element.164), channel_id=1, source_target_pairs={{0,3},{1,0},{2,1},{3,2},{4,7},{5,4},{6,5},{7,6},{8,11},{9,8},{10,9... | collective-permute-start | bytes 387080 | tf_op jit(solution)/shard_map/ppermute | solution.py:357
  233.5 20.4 %collective-permute-start.43 = (bf16[4,224,768]{2,1,0:T(8,128)(2,1)S(1)}, bf16[4,224,768]{2,1,0:T(8,128)(2,1)S(1)}, u32[]{:S(2)}, u32[]{:S(2)}) collective-permute-start(bf16[4,224,768]{2,1,0:T(8,128)(2,1)S(1)} %pad_maximum_fusion), channel_id=1, source_target_pairs={{0,4},{4,0},{8,12},{12,8},{16,20},{20,16},{24,28},{28,24},{1,5},{5... | collective-permute-start | bytes 4128776 | tf_op jit(solution)/shard_map/ppermute | solution.py:353
  (72 other events, 655.3 us)

commit v2 on v1

--- a/solution.py
+++ b/solution.py
@@ -668,9 +668,9 @@
         at = slice(t * OWN, (t + 1) * OWN)
         token_part = dot(mixed[at, :], w_held[...], NT)
         if t == 0:
-            near_ref[at, :] = token_part + first_held[...]
+            near_ref[at, :] = (token_part + first_held[...]).astype(BF16)
         elif t == 1:
-            near_ref[at, :] = token_part
+            near_ref[at, :] = token_part.astype(BF16)
         else:
             far_ref[(t - 2) * OWN : (t - 1) * OWN, :] = token_part.astype(BF16)
         if t == 3:
@@ -1181,13 +1181,11 @@
         (SM, SM, SM, HB, HB, HB, VM, *[HB] * 8),
         [
             *[((LINE, HALF + 16, 3 * WIDE), BF16)] * 2,
-            ((2 * OWN, WIDTH), F32),
-            ((2 * OWN, WIDTH), BF16),
+            *[((2 * OWN, WIDTH), BF16)] * 2,
         ],
         [
             *[pltpu.VMEM((LINE, HALF + 16, 3 * WIDE), BF16)] * 2,
-            pltpu.VMEM((2 * OWN, WIDTH), F32),
-            pltpu.VMEM((2 * OWN, WIDTH), BF16),
+            *[pltpu.VMEM((2 * OWN, WIDTH), BF16)] * 2,
             *[pltpu.VMEM((SLOTS, PAD), BF16)] * 3,
             pltpu.VMEM((WIDTH, 3 * PAD), BF16),
             *[pltpu.VMEM((2 * OWN, WIDTH), BF16)] * 2,
@@ -1256,7 +1254,7 @@
     ]
     qkv_part = sum_parts(turn_parts(qkv_parts))
 
-    near_sum = (token_near + plane_swap(token_far, 1).astype(F32)).reshape(4, SPAN, WIDTH)
+    near_sum = (token_near.astype(F32) + plane_swap(token_far, 1).astype(F32)).reshape(4, SPAN, WIDTH)
     pair = near_sum[:2] + plane_swap(near_sum[2:].astype(BF16), 2).astype(F32)
     for_other = plane_swap(pair[1].astype(BF16), 4)
     for_mine, for_other = pair[0], for_other.astype(F32)

time: 265 us -> 264 us (level)
  other arithmetic: 10.8 us -> 7.59 us
  waiting for transfers between devices: 110 us -> 113 us
    unnamed x88 -> x90, local copies, waits for them, and re-layouts: 5.66 us -> 5.63 us
  transfers between devices with their start and end apart: 52 -> 52, of which waited for: 26 -> 26; matrix products, arithmetic and copies ran while one was open for 4% -> 3% of each run, Pallas kernels for 27% -> 28%
where the time goes in v2:
time: 264 us; the launch traced here: 259 us
  waiting for transfers between devices  113 us (43%)
  Pallas kernels  77.9 us (30%)
  starting transfers between devices  50.1 us (19%)
  local copies, waits for them, and re-layouts  9.47 us (4%)
  other arithmetic  7.59 us (3%)
    pallas_call x10, Pallas kernels, call(): pl.pallas_call(kernel, out_shape=shapes, in_specs=list(spaces), out_specs...  77.9 us
    ppermute x9, waiting for transfers between devices, line_turn(): lax.ppermute(array, 'wa', [(i, (i + step) % LINE) for i in range(LINE)])  52.2 us
    ppermute x42, waiting for transfers between devices, plane_swap(): return lax.ppermute(array, 'ctx', [(i, i ^ bits) for i in range(PLANE)])  49.3 us
    ppermute x42, starting transfers between devices, plane_swap(): return lax.ppermute(array, 'ctx', [(i, i ^ bits) for i in range(PLANE)])  34.9 us
    ppermute x9, starting transfers between devices, line_turn(): lax.ppermute(array, 'wa', [(i, (i + step) % LINE) for i in range(LINE)])  13.6 us
    ppermute x1, waiting for transfers between devices, relay(): return lax.ppermute(passed, 'ctx', pairs)  11.2 us
    unnamed x90, local copies, waits for them, and re-layouts  5.63 us
  transfers between devices with their start and end apart: 52, of which 26 were waited for; matrix products, arithmetic and copies ran while one was open for 3% of the time, Pallas kernels for 28%

profile of v2, /device:TPU:8, one launch (start us, length us, event | category | flops | bytes accessed | tf_op | source)
XLA Modules:
  0.0 259.4 jit_solution(10641140248305605810)
XLA Ops:
  2.5 4.4 %cut.1 = (bf16[192,576]{1,0:T(8,128)(2,1)}, bf16[8,192,384]{2,1,0:T(8,128)(2,1)}, bf16[624,384]{1,0:T(8,128)(2,1)}) custom-call(s32[2]{0:T(128)} %pad_add_fusion.scal, bf16[8,192]{1,0:T(8,128)(2,1)} %vectors.2, bf16[1,768]{1,0:T(2,128)(2,1)} %reshape.73.bias, bf16[192,128]{1,0:T(8,128)(2,1)} %proj_shard.1, bf16[192,2304]{1,0:T(8,128)(2,1)} %qkv.1, ...), custom_call_target="tpu_custom_call" | custom-call | flops 3000000000 | bytes 1 | tf_op jit(solution)/shard_map/cut/pallas_call | solution.py:383
  7.0 3.0 %collective-permute-start.1 = (bf16[624,384]{1,0:T(8,128)(2,1)}, bf16[624,384]{1,0:T(8,128)(2,1)S(1)}, u32[]{:S(2)}, u32[]{:S(2)}) collective-permute-start(bf16[624,384]{1,0:T(8,128)(2,1)} %get-tuple-element.89.own), channel_id=1, source_target_pairs={{0,2},{1,3},{2,0},{3,1},{4,6},{5,7},{6,4},{7,5},{8,10},{9,11},{10,... | collective-permute-start | bytes 1437704 | tf_op jit(solution)/shard_map/ppermute | solution.py:357
  10.0 2.5 collective-permute-start
  15.5 4.9 %collective-permute-done.4 = bf16[128,768]{1,0:T(8,128)(2,1)S(1)} collective-permute-done((bf16[128,768]{1,0:T(8,128)(2,1)S(1)}, bf16[128,768]{1,0:T(8,128)(2,1)S(1)}, u32[]{:S(2)}, u32[]{:S(2)}) %collective-permute-start.4) | collective-permute-done | bytes 196640 | tf_op jit(solution)/shard_map/ppermute | solution.py:353
  24.1 2.8 %collective-permute-done.3 = bf16[128,768]{1,0:T(8,128)(2,1)S(1)} collective-permute-done((bf16[128,768]{1,0:T(8,128)(2,1)S(1)}, bf16[128,768]{1,0:T(8,128)(2,1)S(1)}, u32[]{:S(2)}, u32[]{:S(2)}) %collective-permute-start.3) | collective-permute-done | bytes 196640 | tf_op jit(solution)/shard_map/ppermute | solution.py:353
  26.9 14.6 %collective-permute-done.2 = bf16[624,384]{1,0:T(8,128)(2,1)S(1)} collective-permute-done((bf16[624,384]{1,0:T(8,128)(2,1)}, bf16[624,384]{1,0:T(8,128)(2,1)S(1)}, u32[]{:S(2)}, u32[]{:S(2)}) %collective-permute-start.2) | collective-permute-done | bytes 479264 | tf_op jit(solution)/shard_map/ppermute | solution.py:357
  41.7 9.4 %collective-permute-done = bf16[624,384]{1,0:T(8,128)(2,1)S(1)} collective-permute-done((bf16[624,384]{1,0:T(8,128)(2,1)}, bf16[624,384]{1,0:T(8,128)(2,1)S(1)}, u32[]{:S(2)}, u32[]{:S(2)}) %collective-permute-start) | collective-permute-done | bytes 479264 | tf_op jit(solution)/shard_map/ppermute | solution.py:357
  56.6 6.2 %collective-permute-done.6.others = bf16[3,160,384]{2,1,0:T(8,128)(2,1)S(1)} collective-permute-done((bf16[3,160,384]{2,1,0:T(8,128)(2,1)S(1)}, bf16[3,160,384]{2,1,0:T(8,128)(2,1)S(1)}, u32[]{:S(2)}, u32[]{:S(2)}) %collective-permute-start.6) | collective-permute-done | bytes 368672 | tf_op jit(solution)/shard_map/ppermute | solution.py:353
  63.6 13.5 %attend.1 = (bf16[1024,256]{1,0:T(8,128)(2,1)}, bf16[1024,256]{1,0:T(8,128)(2,1)}, bf16[1024,256]{1,0:T(8,128)(2,1)}, bf16[768,768]{1,0:T(8,128)(2,1)}, bf16[256...) custom-call(s32[2]{0:T(128)} %pad_add_fusion.scal, ...), custom_call_target="tpu_custom_call" | custom-call | flops 12000000000 | bytes 1 | tf_op jit(solution)/shard_map/attend/pallas_call | solution.py:383
  78.7 5.1 %collective-permute-done.10.p1 = bf16[3,432,384]{2,1,0:T(8,128)(2,1)S(1)} collective-permute-done((bf16[3,432,384]{2,1,0:T(8,128)(2,1)S(1)}, bf16[3,432,384]{2,1,0:T(8,128)(2,1)S(1)}, u32[]{:S(2)}, u32[]{:S(2)}) %collective-permute-start.10) | collective-permute-done | bytes 995360 | tf_op jit(solution)/shard_map/ppermute | solution.py:353
  88.1 11.2 %collective-permute-done.12.p3 = bf16[3,432,384]{2,1,0:T(8,128)(2,1)S(1)} collective-permute-done((bf16[3,432,384]{2,1,0:T(8,128)(2,1)S(1)}, bf16[3,432,384]{2,1,0:T(8,128)(2,1)S(1)}, u32[]{:S(2)}, u32[]{:S(2)}) %collective-permute-start.12) | collective-permute-done | bytes 995360 | tf_op jit(solution)/shard_map/ppermute | solution.py:367
  103.8 2.5 collective-permute-start.21
  107.4 17.7 %middle.1 = (bf16[256,128]{1,0:T(8,128)(2,1)S(1)}, bf16[256,768]{1,0:T(8,128)(2,1)S(1)}, f32[256,768]{1,0:T(8,128)S(1)}, bf16[256,256]{1,0:T(8,128)(2,1)S(1)}, b...) custom-call(s32[2]{0:T(128)S(1)} %copy-done.19, ...), custom_call_target="tpu_custom_call" | custom-call | flops 16999999488 | bytes 1 | tf_op jit(solution)/shard_map/middle/pallas_call | solution.py:383
  132.7 4.2 %collective-permute-done.28.g1 = bf16[2,256,256]{2,1,0:T(8,128)(2,1)S(1)} collective-permute-done((bf16[2,256,256]{2,1,0:T(8,128)(2,1)S(1)}, bf16[2,256,256]{2,1,0:T(8,128)(2,1)S(1)}, u32[]{:S(2)}, u32[]{:S(2)}) %collective-permute-start.28) | collective-permute-done | bytes 262176 | tf_op jit(solution)/shard_map/ppermute | solution.py:353
  140.4 18.8 %attend_back.1 = (bf16[4,112,576]{2,1,0:T(8,128)(2,1)}, bf16[4,112,576]{2,1,0:T(8,128)(2,1)}, bf16[512,768]{1,0:T(8,128)(2,1)}, bf16[512,768]{1,0:T(8,128)(2,1)}) custom-call(s32[2]{0:T(128)} %pad_add_fusion.scal, s32[8]{0:T(128)} %lengths.5, s32[8,8]{1,0:T(8,128)} %deal.5, bf16[1024,256]{1,0:T(8,128)(2,1)} %get-tuple-element.118.q_ref, ...), custom_call_target="tpu_custom_call" | custom-call | flops 17999998976 | bytes 1 | tf_op jit(solution)/shard_map/attend_back/pallas_call | solution.py:383
  160.1 7.6 %slice_other.1 = bf16[4,192,768]{2,1,0:T(8,128)(2,1)} custom-call(s32[2]{0:T(128)} %pad_add_fusion.scal, f32[8,384]{1,0:T(8,128)} %copy-done.22, bf16[3,432,384]{2,1,0:T(8,128)(2,1)} %copy-done.6, bf16[8,192,384]{2,1,0:T(8,128)(2,1)} %get-tuple-element.110.ups, bf16[768,768]{1,0:T(8,128)(2,1)} %down.7, bf16[256,768]{1,0:T(8,128)(2,1)} %copy-done.12, ...), custom_call_target="tpu_custom_call" | custom-call | flops 3000000000 | bytes 1 | tf_op jit(solution)/shard_map/slice_other/pallas_call | solution.py:383
  169.5 7.5 %slice_mine.1 = bf16[4,192,768]{2,1,0:T(8,128)(2,1)} custom-call(s32[2]{0:T(128)} %pad_add_fusion.scal, f32[8,384]{1,0:T(8,128)} %copy-done.22, bf16[3,432,384]{2,1,0:T(8,128)(2,1)} %copy-done, bf16[8,192,384]{2,1,0:T(8,128)(2,1)} %get-tuple-element.110.ups, bf16[768,768]{1,0:T(8,128)(2,1)} %down.7, bf16[256,768]{1,0:T(8,128)(2,1)} %copy-done.12, ...), custom_call_target="tpu_custom_call" | custom-call | flops 3000000000 | bytes 1 | tf_op jit(solution)/shard_map/slice_mine/pallas_call | solution.py:383
  179.5 2.4 collective-permute-start.37
  185.3 20.0 %collective-permute-done.37 = bf16[224,768]{1,0:T(8,128)(2,1)S(1)} collective-permute-done((bf16[224,768]{1,0:T(8,128)(2,1)}, bf16[224,768]{1,0:T(8,128)(2,1)S(1)}, u32[]{:S(2)}, u32[]{:S(2)}) %collective-permute-start.37) | collective-permute-done | bytes 344096 | tf_op jit(solution)/shard_map/ppermute | solution.py:357
  205.3 6.6 %collective-permute-done.38 = bf16[224,768]{1,0:T(8,128)(2,1)S(1)} collective-permute-done((bf16[224,768]{1,0:T(8,128)(2,1)}, bf16[224,768]{1,0:T(8,128)(2,1)S(1)}, u32[]{:S(2)}, u32[]{:S(2)}) %collective-permute-start.38) | collective-permute-done | bytes 344096 | tf_op jit(solution)/shard_map/ppermute | solution.py:357
  219.8 5.7 %collective-permute-done.42.p3 = bf16[224,768]{1,0:T(8,128)(2,1)S(1)} collective-permute-done((bf16[224,768]{1,0:T(8,128)(2,1)S(1)}, bf16[224,768]{1,0:T(8,128)(2,1)S(1)}, u32[]{:S(2)}, u32[]{:S(2)}) %collective-permute-start.42) | collective-permute-done | bytes 344096 | tf_op jit(solution)/shard_map/ppermute | solution.py:353
  227.4 3.5 %collective-permute-done.41.p2 = bf16[224,768]{1,0:T(8,128)(2,1)S(1)} collective-permute-done((bf16[224,768]{1,0:T(8,128)(2,1)S(1)}, bf16[224,768]{1,0:T(8,128)(2,1)S(1)}, u32[]{:S(2)}, u32[]{:S(2)}) %collective-permute-start.41) | collective-permute-done | bytes 344096 | tf_op jit(solution)/shard_map/ppermute | solution.py:353
  236.0 7.1 %collective-permute-done.32 = bf16[2,128,768]{2,1,0:T(8,128)(2,1)S(1)} collective-permute-done((bf16[2,128,768]{2,1,0:T(8,128)(2,1)S(1)}, bf16[2,128,768]{2,1,0:T(8,128)(2,1)S(1)}, u32[]{:S(2)}, u32[]{:S(2)}) %collective-permute-start.32) | collective-permute-done | bytes 393248 | tf_op jit(solution)/shard_map/ppermute | solution.py:353
  252.5 3.9 %rest_shard.1 = (f32[192,3072]{1,0:T(8,128)}, f32[768,768]{1,0:T(8,128)}, f32[192,768]{1,0:T(8,128)}, f32[192,128]{1,0:T(8,128)}, f32[8,192]{1,0:T(8,128)S(1)}, /*index=5*/f32[8,96]{1,0:T(8,128)S(1)}) custom-call(s32[2]{0:T(128)S(1)} %copy-done.20, bf16[224,768]{1,0:T(8,128)(2,1)S(1)} %add_convert_fusion.1.p0, ...), custom_call_target="tpu_custom_call" | custom-call | flops 4000000000 | bytes 1 | tf_op jit(solution)/shard_map/rest_shard/pallas_call | solution.py:383
  (223 shorter events, 72.7 us)
Async XLA Ops:
  6.9 34.6 %collective-permute-start.2 = (bf16[624,384]{1,0:T(8,128)(2,1)}, bf16[624,384]{1,0:T(8,128)(2,1)S(1)}, u32[]{:S(2)}, u32[]{:S(2)}) collective-permute-start(bf16[624,384]{1,0:T(8,128)(2,1)} %get-tuple-element.89.own), channel_id=1, source_target_pairs={{0,3},{1,0},{2,1},{3,2},{4,7},{5,4},{6,5},{7,6},{8,11},{9,8},{10,9... | collective-permute-start | bytes 1437704 | tf_op jit(solution)/shard_map/ppermute | solution.py:357
  7.0 34.7 %collective-permute-start.1 = (bf16[624,384]{1,0:T(8,128)(2,1)}, bf16[624,384]{1,0:T(8,128)(2,1)S(1)}, u32[]{:S(2)}, u32[]{:S(2)}) collective-permute-start(bf16[624,384]{1,0:T(8,128)(2,1)} %get-tuple-element.89.own), channel_id=1, source_target_pairs={{0,2},{1,3},{2,0},{3,1},{4,6},{5,7},{6,4},{7,5},{8,10},{9,11},{10,... | collective-permute-start | bytes 1437704 | tf_op jit(solution)/shard_map/ppermute | solution.py:357
  10.0 41.1 %collective-permute-start = (bf16[624,384]{1,0:T(8,128)(2,1)}, bf16[624,384]{1,0:T(8,128)(2,1)S(1)}, u32[]{:S(2)}, u32[]{:S(2)}) collective-permute-start(bf16[624,384]{1,0:T(8,128)(2,1)} %get-tuple-element.89.own), channel_id=1, source_target_pairs={{0,1},{1,2},{2,3},{3,0},{4,5},{5,6},{6,7},{7,4},{8,9},{9,10},{10,1... | collective-permute-start | bytes 1437704 | tf_op jit(solution)/shard_map/ppermute | solution.py:357
  23.6 33.0 %collective-permute-start.8 = (bf16[128,128]{1,0:T(8,128)(2,1)S(1)}, bf16[128,128]{1,0:T(8,128)(2,1)S(1)}, u32[]{:S(2)}, u32[]{:S(2)}) collective-permute-start(bf16[128,128]{1,0:T(8,128)(2,1)S(1)} %get-tuple-element.175), channel_id=1, source_target_pairs={{0,16},{4,20},{8,24},{12,28},{16,0},{20,4},{24,8},{28,12},{1,17},{... | collective-permute-start | bytes 98312 | tf_op jit(solution)/shard_map/ppermute | solution.py:353
  53.3 30.5 %collective-permute-start.10 = (bf16[3,432,384]{2,1,0:T(8,128)(2,1)S(1)}, bf16[3,432,384]{2,1,0:T(8,128)(2,1)S(1)}, u32[]{:S(2)}, u32[]{:S(2)}) collective-permute-start(bf16[3,432,384]{2,1,0:T(8,128)(2,1)S(1)} %pad_maximum_fusion.1.p0.turns), channel_id=1, source_target_pairs={{0,16},{4,20},{8,24},{12,28},{16,0},{20,4},{24,8},{28,12},{1,17},{... | collective-permute-start | bytes 2985992 | tf_op jit(solution)/shard_map/ppermute | solution.py:353
  53.9 29.9 %collective-permute-start.9 = (bf16[3,432,384]{2,1,0:T(8,128)(2,1)S(1)}, bf16[3,432,384]{2,1,0:T(8,128)(2,1)S(1)}, u32[]{:S(2)}, u32[]{:S(2)}) collective-permute-start(bf16[3,432,384]{2,1,0:T(8,128)(2,1)S(1)} %pad_maximum_fusion.1.p0.turns), channel_id=1, source_target_pairs={{0,8},{4,12},{8,0},{12,4},{16,24},{20,28},{24,16},{28,20},{1,9},{5... | collective-permute-start | bytes 2985992 | tf_op jit(solution)/shard_map/ppermute | solution.py:353
  85.0 14.3 %collective-permute-start.12 = (bf16[3,432,384]{2,1,0:T(8,128)(2,1)S(1)}, bf16[3,432,384]{2,1,0:T(8,128)(2,1)S(1)}, u32[]{:S(2)}, u32[]{:S(2)}) collective-permute-start(bf16[3,432,384]{2,1,0:T(8,128)(2,1)S(1)} %broadcast_select_fusion), channel_id=1, source_target_pairs={{0,8},{4,20},{8,0},{12,28},{16,24},{20,4},{24,16},{28,12},{1,9},{5... | collective-permute-start | bytes 2985992 | tf_op jit(solution)/shard_map/ppermute | solution.py:367
  103.8 22.8 %collective-permute-start.21 = (bf16[256,768]{1,0:T(8,128)(2,1)S(1)}, bf16[256,768]{1,0:T(8,128)(2,1)S(1)}, u32[]{:S(2)}, u32[]{:S(2)}) collective-permute-start(bf16[256,768]{1,0:T(8,128)(2,1)S(1)} %get-tuple-element.133.n0), channel_id=1, source_target_pairs={{0,24},{4,28},{8,16},{12,20},{16,8},{20,12},{24,0},{28,4},{1,25},{... | collective-permute-start | bytes 1179656 | tf_op jit(solution)/shard_map/ppermute | solution.py:353
  106.3 20.3 %collective-permute-start.20 = (bf16[256,768]{1,0:T(8,128)(2,1)S(1)}, bf16[256,768]{1,0:T(8,128)(2,1)S(1)}, u32[]{:S(2)}, u32[]{:S(2)}) collective-permute-start(bf16[256,768]{1,0:T(8,128)(2,1)S(1)} %get-tuple-element.133.n0), channel_id=1, source_target_pairs={{0,8},{4,12},{8,0},{12,4},{16,24},{20,28},{24,16},{28,20},{1,9},{5... | collective-permute-start | bytes 1179656 | tf_op jit(solution)/shard_map/ppermute | solution.py:353
  106.9 19.8 %collective-permute-start.19 = (bf16[256,768]{1,0:T(8,128)(2,1)S(1)}, bf16[256,768]{1,0:T(8,128)(2,1)S(1)}, u32[]{:S(2)}, u32[]{:S(2)}) collective-permute-start(bf16[256,768]{1,0:T(8,128)(2,1)S(1)} %get-tuple-element.133.n0), channel_id=1, source_target_pairs={{0,16},{4,20},{8,24},{12,28},{16,0},{20,4},{24,8},{28,12},{1,17},{... | collective-permute-start | bytes 1179656 | tf_op jit(solution)/shard_map/ppermute | solution.py:353
  129.2 29.9 %collective-permute-start.26 = (bf16[256,768]{1,0:T(8,128)(2,1)S(1)}, bf16[256,768]{1,0:T(8,128)(2,1)S(1)}, u32[]{:S(2)}, u32[]{:S(2)}) collective-permute-start(bf16[256,768]{1,0:T(8,128)(2,1)S(1)} %get-tuple-element.141.d0), channel_id=1, source_target_pairs={{0,24},{4,28},{8,16},{12,20},{16,8},{20,12},{24,0},{28,4},{1,25},{... | collective-permute-start | bytes 1179656 | tf_op jit(solution)/shard_map/ppermute | solution.py:353
  130.7 28.4 %collective-permute-start.25 = (bf16[256,768]{1,0:T(8,128)(2,1)S(1)}, bf16[256,768]{1,0:T(8,128)(2,1)S(1)}, u32[]{:S(2)}, u32[]{:S(2)}) collective-permute-start(bf16[256,768]{1,0:T(8,128)(2,1)S(1)} %get-tuple-element.141.d0), channel_id=1, source_target_pairs={{0,8},{4,12},{8,0},{12,4},{16,24},{20,28},{24,16},{28,20},{1,9},{5... | collective-permute-start | bytes 1179656 | tf_op jit(solution)/shard_map/ppermute | solution.py:353
  132.2 27.0 %collective-permute-start.24 = (bf16[256,768]{1,0:T(8,128)(2,1)S(1)}, bf16[256,768]{1,0:T(8,128)(2,1)S(1)}, u32[]{:S(2)}, u32[]{:S(2)}) collective-permute-start(bf16[256,768]{1,0:T(8,128)(2,1)S(1)} %get-tuple-element.141.d0), channel_id=1, source_target_pairs={{0,16},{4,20},{8,24},{12,28},{16,0},{20,4},{24,8},{28,12},{1,17},{... | collective-permute-start | bytes 1179656 | tf_op jit(solution)/shard_map/ppermute | solution.py:353
  138.2 29.6 %collective-permute-start.34 = (bf16[4,64,768]{2,1,0:T(8,128)(2,1)S(1)}, bf16[4,64,768]{2,1,0:T(8,128)(2,1)S(1)}, u32[]{:S(2)}, u32[]{:S(2)}) collective-permute-start(bf16[4,64,768]{2,1,0:T(8,128)(2,1)S(1)} %dynamic-slice_bitcast_fusion), channel_id=1, source_target_pairs={{0,8},{4,12},{8,0},{12,4},{16,24},{20,28},{24,16},{28,20},{1,9},{5... | collective-permute-start | bytes 1179656 | tf_op jit(solution)/shard_map/ppermute | solution.py:353
  179.5 25.9 %collective-permute-start.37 = (bf16[224,768]{1,0:T(8,128)(2,1)}, bf16[224,768]{1,0:T(8,128)(2,1)S(1)}, u32[]{:S(2)}, u32[]{:S(2)}) collective-permute-start(bf16[224,768]{1,0:T(8,128)(2,1)} %pad_maximum_fusion.5), channel_id=1, source_target_pairs={{0,1},{1,2},{2,3},{3,0},{4,5},{5,6},{6,7},{7,4},{8,9},{9,10},{10,1... | collective-permute-start | bytes 1032200 | tf_op jit(solution)/shard_map/ppermute | solution.py:357
  182.6 29.4 %collective-permute-start.38 = (bf16[224,768]{1,0:T(8,128)(2,1)}, bf16[224,768]{1,0:T(8,128)(2,1)S(1)}, u32[]{:S(2)}, u32[]{:S(2)}) collective-permute-start(bf16[224,768]{1,0:T(8,128)(2,1)} %pad_maximum_fusion.6), channel_id=1, source_target_pairs={{0,2},{1,3},{2,0},{3,1},{4,6},{5,7},{6,4},{7,5},{8,10},{9,11},{10,... | collective-permute-start | bytes 1032200 | tf_op jit(solution)/shard_map/ppermute | solution.py:357
  184.4 29.0 %collective-permute-start.39 = (bf16[224,768]{1,0:T(8,128)(2,1)}, bf16[224,768]{1,0:T(8,128)(2,1)S(1)}, u32[]{:S(2)}, u32[]{:S(2)}) collective-permute-start(bf16[224,768]{1,0:T(8,128)(2,1)} %pad_maximum_fusion.7), channel_id=1, source_target_pairs={{0,3},{1,0},{2,1},{3,2},{4,7},{5,4},{6,5},{7,6},{8,11},{9,8},{10,9... | collective-permute-start | bytes 1032200 | tf_op jit(solution)/shard_map/ppermute | solution.py:357
  184.8 32.5 %collective-permute-start.31 = (bf16[512,768]{1,0:T(8,128)(2,1)}, bf16[512,768]{1,0:T(8,128)(2,1)S(1)}, u32[]{:S(2)}, u32[]{:S(2)}) collective-permute-start(bf16[512,768]{1,0:T(8,128)(2,1)} %get-tuple-element.132), channel_id=1, source_target_pairs={{0,4},{4,0},{8,12},{12,8},{16,20},{20,16},{24,28},{28,24},{1,5},{5... | collective-permute-start | bytes 2359304 | tf_op jit(solution)/shard_map/ppermute | solution.py:353
  184.8 32.3 %collective-permute-start.44 = (bf16[4,112,576]{2,1,0:T(8,128)(2,1)}, bf16[4,112,576]{2,1,0:T(8,128)(2,1)S(1)}, u32[]{:S(2)}, u32[]{:S(2)}) collective-permute-start(bf16[4,112,576]{2,1,0:T(8,128)(2,1)} %get-tuple-element.151), channel_id=1, source_target_pairs={{0,16},{4,20},{8,24},{12,28},{16,0},{20,4},{24,8},{28,12},{1,17},{... | collective-permute-start | bytes 1548296 | tf_op jit(solution)/shard_map/ppermute | solution.py:353
  214.1 16.9 %collective-permute-start.41 = (bf16[224,768]{1,0:T(8,128)(2,1)S(1)}, bf16[224,768]{1,0:T(8,128)(2,1)S(1)}, u32[]{:S(2)}, u32[]{:S(2)}) collective-permute-start(bf16[224,768]{1,0:T(8,128)(2,1)S(1)} %add_convert_fusion.1.p0), channel_id=1, source_target_pairs={{0,8},{4,12},{8,0},{12,4},{16,24},{20,28},{24,16},{28,20},{1,9},{5... | collective-permute-start | bytes 1032200 | tf_op jit(solution)/shard_map/ppermute | solution.py:353
  215.6 16.3 %collective-permute-start.40 = (bf16[224,768]{1,0:T(8,128)(2,1)S(1)}, bf16[224,768]{1,0:T(8,128)(2,1)S(1)}, u32[]{:S(2)}, u32[]{:S(2)}) collective-permute-start(bf16[224,768]{1,0:T(8,128)(2,1)S(1)} %add_convert_fusion.1.p0), channel_id=1, source_target_pairs={{0,16},{4,20},{8,24},{12,28},{16,0},{20,4},{24,8},{28,12},{1,17},{... | collective-permute-start | bytes 1032200 | tf_op jit(solution)/shard_map/ppermute | solution.py:353
  217.2 14.9 %collective-permute-start.45 = (bf16[112,576]{1,0:T(8,128)(2,1)S(1)}, bf16[112,576]{1,0:T(8,128)(2,1)S(1)}, u32[]{:S(2)}, u32[]{:S(2)}) collective-permute-start(bf16[112,576]{1,0:T(8,128)(2,1)S(1)} %get-tuple-element.163), channel_id=1, source_target_pairs={{0,1},{1,2},{2,3},{3,0},{4,5},{5,6},{6,7},{7,4},{8,9},{9,10},{10,1... | collective-permute-start | bytes 387080 | tf_op jit(solution)/shard_map/ppermute | solution.py:357
  217.3 16.1 %collective-permute-start.47 = (bf16[112,576]{1,0:T(8,128)(2,1)S(1)}, bf16[112,576]{1,0:T(8,128)(2,1)S(1)}, u32[]{:S(2)}, u32[]{:S(2)}) collective-permute-start(bf16[112,576]{1,0:T(8,128)(2,1)S(1)} %get-tuple-element.164), channel_id=1, source_target_pairs={{0,3},{1,0},{2,1},{3,2},{4,7},{5,4},{6,5},{7,6},{8,11},{9,8},{10,9... | collective-permute-start | bytes 387080 | tf_op jit(solution)/shard_map/ppermute | solution.py:357
  232.1 20.4 %collective-permute-start.43 = (bf16[4,224,768]{2,1,0:T(8,128)(2,1)S(1)}, bf16[4,224,768]{2,1,0:T(8,128)(2,1)S(1)}, u32[]{:S(2)}, u32[]{:S(2)}) collective-permute-start(bf16[4,224,768]{2,1,0:T(8,128)(2,1)S(1)} %pad_maximum_fusion), channel_id=1, source_target_pairs={{0,4},{4,0},{8,12},{12,8},{16,20},{20,16},{24,28},{28,24},{1,5},{5... | collective-permute-start | bytes 4128776 | tf_op jit(solution)/shard_map/ppermute | solution.py:353
  (73 other events, 659.2 us)

commit v3 on v2

--- a/solution.py
+++ b/solution.py
@@ -440,7 +440,8 @@
     for copy in copies:
         copy.start()
     rows = [vectors[...].astype(F32)]
-    rows += [bias[:, a * SHARD : (a + 1) * SHARD].astype(F32) for a in range(LINE)]
+    flat = bias[...].astype(F32).reshape(1, WIDTH)
+    rows += [flat[:, a * SHARD : (a + 1) * SHARD] for a in range(LINE)]
     rows = jnp.concatenate(rows + [jnp.zeros((4, SHARD), F32)])
     own_ref[PARTS + COLS : PARTS + COLS + 16, :SHARD] = rows.astype(BF16)
     own_ref[PARTS + COLS : PARTS + COLS + 16, SHARD:] = jnp.zeros((16, SLICE - SHARD), BF16)
@@ -965,7 +966,8 @@
         @pl.when(line == z)
         def _():
             rows_ref[...] = small[:8, z * SHARD : (z + 1) * SHARD]
-            bias_ref[...] = small[8:, z * PIECE : (z + 1) * PIECE]
+            flat = [small[8 + k : 9 + k, z * PIECE : (z + 1) * PIECE] for k in range(PLANE)]
+            bias_ref[...] = jnp.concatenate(flat, axis=1).reshape(WIDTH)
 
 
 def qkv_shard_kernel(scal, late, p0, p1, p2, p3, far, qkv_ref, rows_ref, held):
@@ -1029,7 +1031,7 @@
 
     own_cols, ups, own_parts = call(
         cut_kernel,
-        (scal, vectors, up_bias.reshape(1, -1), proj_weight)
+        (scal, vectors, up_bias, proj_weight)
         + (qkv_weight, up_weight, down_weight, out_weight),
         (SM, VM, VM, VM, HB, HB, HB, HB),
         [
@@ -1271,12 +1273,12 @@
             ((SHARD, WIDTH), F32),
             ((SHARD, EMBED), F32),
             ((8, SHARD), F32),
-            ((PLANE, PIECE), F32),
+            ((PLANE * PIECE,), F32),
         ],
         [pltpu.VMEM((PLANE, 2 * HALF + 32, WIDTH), BF16)],
         name="rest_shard",
     )
-    bias_grad = bias_rows.reshape(-1)
+    bias_grad = bias_rows
     qkv_grad, vectors_grad = call(
         qkv_shard_kernel,
         (scal, late_rows, *gather_plane(qkv_part)),

time: 264 us -> 262 us (level)
  no operation moved by 1% of the time
where the time goes in v3:
time: 262 us; the launch traced here: 257 us
  waiting for transfers between devices  113 us (43%)
  Pallas kernels  77.9 us (30%)
  starting transfers between devices  50.1 us (19%)
  other arithmetic  7.59 us (3%)
  local copies, waits for them, and re-layouts  7.54 us (3%)
    pallas_call x10, Pallas kernels, call(): pl.pallas_call(kernel, out_shape=shapes, in_specs=list(spaces), out_specs...  77.9 us
    ppermute x9, waiting for transfers between devices, line_turn(): lax.ppermute(array, 'wa', [(i, (i + step) % LINE) for i in range(LINE)])  52.2 us
    ppermute x42, waiting for transfers between devices, plane_swap(): return lax.ppermute(array, 'ctx', [(i, i ^ bits) for i in range(PLANE)])  49.3 us
    ppermute x42, starting transfers between devices, plane_swap(): return lax.ppermute(array, 'ctx', [(i, i ^ bits) for i in range(PLANE)])  34.9 us
    ppermute x9, starting transfers between devices, line_turn(): lax.ppermute(array, 'wa', [(i, (i + step) % LINE) for i in range(LINE)])  13.6 us
    ppermute x1, waiting for transfers between devices, relay(): return lax.ppermute(passed, 'ctx', pairs)  11.2 us
    unnamed x90, local copies, waits for them, and re-layouts  5.63 us
  transfers between devices with their start and end apart: 52, of which 26 were waited for; matrix products, arithmetic and copies ran while one was open for 3% of the time, Pallas kernels for 28%

profile of v3, /device:TPU:8, one launch (start us, length us, event | category | flops | bytes accessed | tf_op | source)
XLA Modules:
  0.0 257.5 jit_solution(131913295607039273)
XLA Ops:
  1.2 4.4 %cut.1 = (bf16[192,576]{1,0:T(8,128)(2,1)}, bf16[8,192,384]{2,1,0:T(8,128)(2,1)}, bf16[624,384]{1,0:T(8,128)(2,1)}) custom-call(s32[2]{0:T(128)} %pad_add_fusion.scal, bf16[8,192]{1,0:T(8,128)(2,1)} %vectors.2, bf16[768]{0:T(1024)(128)(2,1)} %bias.1, bf16[192,128]{1,0:T(8,128)(2,1)} %proj_shard.1, bf16[192,2304]{1,0:T(8,128)(2,1)} %qkv.1, ...), custom_call_target="tpu_custom_call" | custom-call | flops 3000000000 | bytes 1 | tf_op jit(solution)/shard_map/cut/pallas_call | solution.py:383
  5.7 3.0 %collective-permute-start.1 = (bf16[624,384]{1,0:T(8,128)(2,1)}, bf16[624,384]{1,0:T(8,128)(2,1)S(1)}, u32[]{:S(2)}, u32[]{:S(2)}) collective-permute-start(bf16[624,384]{1,0:T(8,128)(2,1)} %get-tuple-element.89.own), channel_id=1, source_target_pairs={{0,2},{1,3},{2,0},{3,1},{4,6},{5,7},{6,4},{7,5},{8,10},{9,11},{10,... | collective-permute-start | bytes 1437704 | tf_op jit(solution)/shard_map/ppermute | solution.py:357
  8.7 2.5 collective-permute-start
  14.3 4.9 %collective-permute-done.4 = bf16[128,768]{1,0:T(8,128)(2,1)S(1)} collective-permute-done((bf16[128,768]{1,0:T(8,128)(2,1)S(1)}, bf16[128,768]{1,0:T(8,128)(2,1)S(1)}, u32[]{:S(2)}, u32[]{:S(2)}) %collective-permute-start.4) | collective-permute-done | bytes 196640 | tf_op jit(solution)/shard_map/ppermute | solution.py:353
  22.9 2.8 %collective-permute-done.3 = bf16[128,768]{1,0:T(8,128)(2,1)S(1)} collective-permute-done((bf16[128,768]{1,0:T(8,128)(2,1)S(1)}, bf16[128,768]{1,0:T(8,128)(2,1)S(1)}, u32[]{:S(2)}, u32[]{:S(2)}) %collective-permute-start.3) | collective-permute-done | bytes 196640 | tf_op jit(solution)/shard_map/ppermute | solution.py:353
  25.7 14.6 %collective-permute-done.2 = bf16[624,384]{1,0:T(8,128)(2,1)S(1)} collective-permute-done((bf16[624,384]{1,0:T(8,128)(2,1)}, bf16[624,384]{1,0:T(8,128)(2,1)S(1)}, u32[]{:S(2)}, u32[]{:S(2)}) %collective-permute-start.2) | collective-permute-done | bytes 479264 | tf_op jit(solution)/shard_map/ppermute | solution.py:357
  40.4 9.4 %collective-permute-done = bf16[624,384]{1,0:T(8,128)(2,1)S(1)} collective-permute-done((bf16[624,384]{1,0:T(8,128)(2,1)}, bf16[624,384]{1,0:T(8,128)(2,1)S(1)}, u32[]{:S(2)}, u32[]{:S(2)}) %collective-permute-start) | collective-permute-done | bytes 479264 | tf_op jit(solution)/shard_map/ppermute | solution.py:357
  55.4 6.2 %collective-permute-done.6.others = bf16[3,160,384]{2,1,0:T(8,128)(2,1)S(1)} collective-permute-done((bf16[3,160,384]{2,1,0:T(8,128)(2,1)S(1)}, bf16[3,160,384]{2,1,0:T(8,128)(2,1)S(1)}, u32[]{:S(2)}, u32[]{:S(2)}) %collective-permute-start.6) | collective-permute-done | bytes 368672 | tf_op jit(solution)/shard_map/ppermute | solution.py:353
  62.3 13.5 %attend.1 = (bf16[1024,256]{1,0:T(8,128)(2,1)}, bf16[1024,256]{1,0:T(8,128)(2,1)}, bf16[1024,256]{1,0:T(8,128)(2,1)}, bf16[768,768]{1,0:T(8,128)(2,1)}, bf16[256...) custom-call(s32[2]{0:T(128)} %pad_add_fusion.scal, ...), custom_call_target="tpu_custom_call" | custom-call | flops 12000000000 | bytes 1 | tf_op jit(solution)/shard_map/attend/pallas_call | solution.py:383
  77.4 5.1 %collective-permute-done.10.p1 = bf16[3,432,384]{2,1,0:T(8,128)(2,1)S(1)} collective-permute-done((bf16[3,432,384]{2,1,0:T(8,128)(2,1)S(1)}, bf16[3,432,384]{2,1,0:T(8,128)(2,1)S(1)}, u32[]{:S(2)}, u32[]{:S(2)}) %collective-permute-start.10) | collective-permute-done | bytes 995360 | tf_op jit(solution)/shard_map/ppermute | solution.py:353
  86.9 11.2 %collective-permute-done.12.p3 = bf16[3,432,384]{2,1,0:T(8,128)(2,1)S(1)} collective-permute-done((bf16[3,432,384]{2,1,0:T(8,128)(2,1)S(1)}, bf16[3,432,384]{2,1,0:T(8,128)(2,1)S(1)}, u32[]{:S(2)}, u32[]{:S(2)}) %collective-permute-start.12) | collective-permute-done | bytes 995360 | tf_op jit(solution)/shard_map/ppermute | solution.py:367
  102.6 2.5 collective-permute-start.21
  106.1 17.7 %middle.1 = (bf16[256,128]{1,0:T(8,128)(2,1)S(1)}, bf16[256,768]{1,0:T(8,128)(2,1)S(1)}, f32[256,768]{1,0:T(8,128)S(1)}, bf16[256,256]{1,0:T(8,128)(2,1)S(1)}, b...) custom-call(s32[2]{0:T(128)S(1)} %copy-done.19, ...), custom_call_target="tpu_custom_call" | custom-call | flops 16999999488 | bytes 1 | tf_op jit(solution)/shard_map/middle/pallas_call | solution.py:383
  131.4 4.2 %collective-permute-done.28.g1 = bf16[2,256,256]{2,1,0:T(8,128)(2,1)S(1)} collective-permute-done((bf16[2,256,256]{2,1,0:T(8,128)(2,1)S(1)}, bf16[2,256,256]{2,1,0:T(8,128)(2,1)S(1)}, u32[]{:S(2)}, u32[]{:S(2)}) %collective-permute-start.28) | collective-permute-done | bytes 262176 | tf_op jit(solution)/shard_map/ppermute | solution.py:353
  139.1 18.8 %attend_back.1 = (bf16[4,112,576]{2,1,0:T(8,128)(2,1)}, bf16[4,112,576]{2,1,0:T(8,128)(2,1)}, bf16[512,768]{1,0:T(8,128)(2,1)}, bf16[512,768]{1,0:T(8,128)(2,1)}) custom-call(s32[2]{0:T(128)} %pad_add_fusion.scal, s32[8]{0:T(128)} %lengths.5, s32[8,8]{1,0:T(8,128)} %deal.5, bf16[1024,256]{1,0:T(8,128)(2,1)} %get-tuple-element.118.q_ref, ...), custom_call_target="tpu_custom_call" | custom-call | flops 17999998976 | bytes 1 | tf_op jit(solution)/shard_map/attend_back/pallas_call | solution.py:383
  158.9 7.6 %slice_other.1 = bf16[4,192,768]{2,1,0:T(8,128)(2,1)} custom-call(s32[2]{0:T(128)} %pad_add_fusion.scal, f32[8,384]{1,0:T(8,128)} %copy-done.22, bf16[3,432,384]{2,1,0:T(8,128)(2,1)} %copy-done.6, bf16[8,192,384]{2,1,0:T(8,128)(2,1)} %get-tuple-element.110.ups, bf16[768,768]{1,0:T(8,128)(2,1)} %down.7, bf16[256,768]{1,0:T(8,128)(2,1)} %copy-done.12, ...), custom_call_target="tpu_custom_call" | custom-call | flops 3000000000 | bytes 1 | tf_op jit(solution)/shard_map/slice_other/pallas_call | solution.py:383
  168.3 7.5 %slice_mine.1 = bf16[4,192,768]{2,1,0:T(8,128)(2,1)} custom-call(s32[2]{0:T(128)} %pad_add_fusion.scal, f32[8,384]{1,0:T(8,128)} %copy-done.22, bf16[3,432,384]{2,1,0:T(8,128)(2,1)} %copy-done, bf16[8,192,384]{2,1,0:T(8,128)(2,1)} %get-tuple-element.110.ups, bf16[768,768]{1,0:T(8,128)(2,1)} %down.7, bf16[256,768]{1,0:T(8,128)(2,1)} %copy-done.12, ...), custom_call_target="tpu_custom_call" | custom-call | flops 3000000000 | bytes 1 | tf_op jit(solution)/shard_map/slice_mine/pallas_call | solution.py:383
  178.2 2.4 collective-permute-start.37
  184.0 20.0 %collective-permute-done.37 = bf16[224,768]{1,0:T(8,128)(2,1)S(1)} collective-permute-done((bf16[224,768]{1,0:T(8,128)(2,1)}, bf16[224,768]{1,0:T(8,128)(2,1)S(1)}, u32[]{:S(2)}, u32[]{:S(2)}) %collective-permute-start.37) | collective-permute-done | bytes 344096 | tf_op jit(solution)/shard_map/ppermute | solution.py:357
  204.1 6.6 %collective-permute-done.38 = bf16[224,768]{1,0:T(8,128)(2,1)S(1)} collective-permute-done((bf16[224,768]{1,0:T(8,128)(2,1)}, bf16[224,768]{1,0:T(8,128)(2,1)S(1)}, u32[]{:S(2)}, u32[]{:S(2)}) %collective-permute-start.38) | collective-permute-done | bytes 344096 | tf_op jit(solution)/shard_map/ppermute | solution.py:357
  218.5 5.7 %collective-permute-done.42.p3 = bf16[224,768]{1,0:T(8,128)(2,1)S(1)} collective-permute-done((bf16[224,768]{1,0:T(8,128)(2,1)S(1)}, bf16[224,768]{1,0:T(8,128)(2,1)S(1)}, u32[]{:S(2)}, u32[]{:S(2)}) %collective-permute-start.42) | collective-permute-done | bytes 344096 | tf_op jit(solution)/shard_map/ppermute | solution.py:353
  226.2 3.5 %collective-permute-done.41.p2 = bf16[224,768]{1,0:T(8,128)(2,1)S(1)} collective-permute-done((bf16[224,768]{1,0:T(8,128)(2,1)S(1)}, bf16[224,768]{1,0:T(8,128)(2,1)S(1)}, u32[]{:S(2)}, u32[]{:S(2)}) %collective-permute-start.41) | collective-permute-done | bytes 344096 | tf_op jit(solution)/shard_map/ppermute | solution.py:353
  234.7 7.1 %collective-permute-done.32 = bf16[2,128,768]{2,1,0:T(8,128)(2,1)S(1)} collective-permute-done((bf16[2,128,768]{2,1,0:T(8,128)(2,1)S(1)}, bf16[2,128,768]{2,1,0:T(8,128)(2,1)S(1)}, u32[]{:S(2)}, u32[]{:S(2)}) %collective-permute-start.32) | collective-permute-done | bytes 393248 | tf_op jit(solution)/shard_map/ppermute | solution.py:353
  251.2 4.0 %rest_shard.1 = (f32[192,3072]{1,0:T(8,128)}, f32[768,768]{1,0:T(8,128)}, f32[192,768]{1,0:T(8,128)}, f32[192,128]{1,0:T(8,128)}, f32[8,192]{1,0:T(8,128)S(1)}, /*index=5*/f32[768]{0:T(1024)}) custom-call(s32[2]{0:T(128)S(1)} %copy-done.20, bf16[224,768]{1,0:T(8,128)(2,1)S(1)} %add_convert_fusion.1.p0, bf16[224,768]{1,0:T(8,128)(2,1)S(1)} %collective-permute-done.40.p1, ...), custom_call_target="tpu_custom_call" | custom-call | flops 4000000000 | bytes 1 | tf_op jit(solution)/shard_map/rest_shard/pallas_call | solution.py:383
  (221 shorter events, 70.8 us)
Async XLA Ops:
  5.6 34.6 %collective-permute-start.2 = (bf16[624,384]{1,0:T(8,128)(2,1)}, bf16[624,384]{1,0:T(8,128)(2,1)S(1)}, u32[]{:S(2)}, u32[]{:S(2)}) collective-permute-start(bf16[624,384]{1,0:T(8,128)(2,1)} %get-tuple-element.89.own), channel_id=1, source_target_pairs={{0,3},{1,0},{2,1},{3,2},{4,7},{5,4},{6,5},{7,6},{8,11},{9,8},{10,9... | collective-permute-start | bytes 1437704 | tf_op jit(solution)/shard_map/ppermute | solution.py:357
  5.7 34.7 %collective-permute-start.1 = (bf16[624,384]{1,0:T(8,128)(2,1)}, bf16[624,384]{1,0:T(8,128)(2,1)S(1)}, u32[]{:S(2)}, u32[]{:S(2)}) collective-permute-start(bf16[624,384]{1,0:T(8,128)(2,1)} %get-tuple-element.89.own), channel_id=1, source_target_pairs={{0,2},{1,3},{2,0},{3,1},{4,6},{5,7},{6,4},{7,5},{8,10},{9,11},{10,... | collective-permute-start | bytes 1437704 | tf_op jit(solution)/shard_map/ppermute | solution.py:357
  8.7 41.1 %collective-permute-start = (bf16[624,384]{1,0:T(8,128)(2,1)}, bf16[624,384]{1,0:T(8,128)(2,1)S(1)}, u32[]{:S(2)}, u32[]{:S(2)}) collective-permute-start(bf16[624,384]{1,0:T(8,128)(2,1)} %get-tuple-element.89.own), channel_id=1, source_target_pairs={{0,1},{1,2},{2,3},{3,0},{4,5},{5,6},{6,7},{7,4},{8,9},{9,10},{10,1... | collective-permute-start | bytes 1437704 | tf_op jit(solution)/shard_map/ppermute | solution.py:357
  22.4 33.0 %collective-permute-start.8 = (bf16[128,128]{1,0:T(8,128)(2,1)S(1)}, bf16[128,128]{1,0:T(8,128)(2,1)S(1)}, u32[]{:S(2)}, u32[]{:S(2)}) collective-permute-start(bf16[128,128]{1,0:T(8,128)(2,1)S(1)} %get-tuple-element.175), channel_id=1, source_target_pairs={{0,16},{4,20},{8,24},{12,28},{16,0},{20,4},{24,8},{28,12},{1,17},{... | collective-permute-start | bytes 98312 | tf_op jit(solution)/shard_map/ppermute | solution.py:353
  52.0 30.5 %collective-permute-start.10 = (bf16[3,432,384]{2,1,0:T(8,128)(2,1)S(1)}, bf16[3,432,384]{2,1,0:T(8,128)(2,1)S(1)}, u32[]{:S(2)}, u32[]{:S(2)}) collective-permute-start(bf16[3,432,384]{2,1,0:T(8,128)(2,1)S(1)} %pad_maximum_fusion.1.p0.turns), channel_id=1, source_target_pairs={{0,16},{4,20},{8,24},{12,28},{16,0},{20,4},{24,8},{28,12},{1,17},{... | collective-permute-start | bytes 2985992 | tf_op jit(solution)/shard_map/ppermute | solution.py:353
  52.6 29.9 %collective-permute-start.9 = (bf16[3,432,384]{2,1,0:T(8,128)(2,1)S(1)}, bf16[3,432,384]{2,1,0:T(8,128)(2,1)S(1)}, u32[]{:S(2)}, u32[]{:S(2)}) collective-permute-start(bf16[3,432,384]{2,1,0:T(8,128)(2,1)S(1)} %pad_maximum_fusion.1.p0.turns), channel_id=1, source_target_pairs={{0,8},{4,12},{8,0},{12,4},{16,24},{20,28},{24,16},{28,20},{1,9},{5... | collective-permute-start | bytes 2985992 | tf_op jit(solution)/shard_map/ppermute | solution.py:353
  83.7 14.3 %collective-permute-start.12 = (bf16[3,432,384]{2,1,0:T(8,128)(2,1)S(1)}, bf16[3,432,384]{2,1,0:T(8,128)(2,1)S(1)}, u32[]{:S(2)}, u32[]{:S(2)}) collective-permute-start(bf16[3,432,384]{2,1,0:T(8,128)(2,1)S(1)} %broadcast_select_fusion), channel_id=1, source_target_pairs={{0,8},{4,20},{8,0},{12,28},{16,24},{20,4},{24,16},{28,12},{1,9},{5... | collective-permute-start | bytes 2985992 | tf_op jit(solution)/shard_map/ppermute | solution.py:367
  102.6 22.8 %collective-permute-start.21 = (bf16[256,768]{1,0:T(8,128)(2,1)S(1)}, bf16[256,768]{1,0:T(8,128)(2,1)S(1)}, u32[]{:S(2)}, u32[]{:S(2)}) collective-permute-start(bf16[256,768]{1,0:T(8,128)(2,1)S(1)} %get-tuple-element.133.n0), channel_id=1, source_target_pairs={{0,24},{4,28},{8,16},{12,20},{16,8},{20,12},{24,0},{28,4},{1,25},{... | collective-permute-start | bytes 1179656 | tf_op jit(solution)/shard_map/ppermute | solution.py:353
  105.1 20.3 %collective-permute-start.20 = (bf16[256,768]{1,0:T(8,128)(2,1)S(1)}, bf16[256,768]{1,0:T(8,128)(2,1)S(1)}, u32[]{:S(2)}, u32[]{:S(2)}) collective-permute-start(bf16[256,768]{1,0:T(8,128)(2,1)S(1)} %get-tuple-element.133.n0), channel_id=1, source_target_pairs={{0,8},{4,12},{8,0},{12,4},{16,24},{20,28},{24,16},{28,20},{1,9},{5... | collective-permute-start | bytes 1179656 | tf_op jit(solution)/shard_map/ppermute | solution.py:353
  105.6 19.8 %collective-permute-start.19 = (bf16[256,768]{1,0:T(8,128)(2,1)S(1)}, bf16[256,768]{1,0:T(8,128)(2,1)S(1)}, u32[]{:S(2)}, u32[]{:S(2)}) collective-permute-start(bf16[256,768]{1,0:T(8,128)(2,1)S(1)} %get-tuple-element.133.n0), channel_id=1, source_target_pairs={{0,16},{4,20},{8,24},{12,28},{16,0},{20,4},{24,8},{28,12},{1,17},{... | collective-permute-start | bytes 1179656 | tf_op jit(solution)/shard_map/ppermute | solution.py:353
  127.9 29.9 %collective-permute-start.26 = (bf16[256,768]{1,0:T(8,128)(2,1)S(1)}, bf16[256,768]{1,0:T(8,128)(2,1)S(1)}, u32[]{:S(2)}, u32[]{:S(2)}) collective-permute-start(bf16[256,768]{1,0:T(8,128)(2,1)S(1)} %get-tuple-element.141.d0), channel_id=1, source_target_pairs={{0,24},{4,28},{8,16},{12,20},{16,8},{20,12},{24,0},{28,4},{1,25},{... | collective-permute-start | bytes 1179656 | tf_op jit(solution)/shard_map/ppermute | solution.py:353
  129.4 28.4 %collective-permute-start.25 = (bf16[256,768]{1,0:T(8,128)(2,1)S(1)}, bf16[256,768]{1,0:T(8,128)(2,1)S(1)}, u32[]{:S(2)}, u32[]{:S(2)}) collective-permute-start(bf16[256,768]{1,0:T(8,128)(2,1)S(1)} %get-tuple-element.141.d0), channel_id=1, source_target_pairs={{0,8},{4,12},{8,0},{12,4},{16,24},{20,28},{24,16},{28,20},{1,9},{5... | collective-permute-start | bytes 1179656 | tf_op jit(solution)/shard_map/ppermute | solution.py:353
  130.9 27.0 %collective-permute-start.24 = (bf16[256,768]{1,0:T(8,128)(2,1)S(1)}, bf16[256,768]{1,0:T(8,128)(2,1)S(1)}, u32[]{:S(2)}, u32[]{:S(2)}) collective-permute-start(bf16[256,768]{1,0:T(8,128)(2,1)S(1)} %get-tuple-element.141.d0), channel_id=1, source_target_pairs={{0,16},{4,20},{8,24},{12,28},{16,0},{20,4},{24,8},{28,12},{1,17},{... | collective-permute-start | bytes 1179656 | tf_op jit(solution)/shard_map/ppermute | solution.py:353
  137.0 29.6 %collective-permute-start.34 = (bf16[4,64,768]{2,1,0:T(8,128)(2,1)S(1)}, bf16[4,64,768]{2,1,0:T(8,128)(2,1)S(1)}, u32[]{:S(2)}, u32[]{:S(2)}) collective-permute-start(bf16[4,64,768]{2,1,0:T(8,128)(2,1)S(1)} %dynamic-slice_bitcast_fusion), channel_id=1, source_target_pairs={{0,8},{4,12},{8,0},{12,4},{16,24},{20,28},{24,16},{28,20},{1,9},{5... | collective-permute-start | bytes 1179656 | tf_op jit(solution)/shard_map/ppermute | solution.py:353
  178.2 25.9 %collective-permute-start.37 = (bf16[224,768]{1,0:T(8,128)(2,1)}, bf16[224,768]{1,0:T(8,128)(2,1)S(1)}, u32[]{:S(2)}, u32[]{:S(2)}) collective-permute-start(bf16[224,768]{1,0:T(8,128)(2,1)} %pad_maximum_fusion.5), channel_id=1, source_target_pairs={{0,1},{1,2},{2,3},{3,0},{4,5},{5,6},{6,7},{7,4},{8,9},{9,10},{10,1... | collective-permute-start | bytes 1032200 | tf_op jit(solution)/shard_map/ppermute | solution.py:357
  181.3 29.4 %collective-permute-start.38 = (bf16[224,768]{1,0:T(8,128)(2,1)}, bf16[224,768]{1,0:T(8,128)(2,1)S(1)}, u32[]{:S(2)}, u32[]{:S(2)}) collective-permute-start(bf16[224,768]{1,0:T(8,128)(2,1)} %pad_maximum_fusion.6), channel_id=1, source_target_pairs={{0,2},{1,3},{2,0},{3,1},{4,6},{5,7},{6,4},{7,5},{8,10},{9,11},{10,... | collective-permute-start | bytes 1032200 | tf_op jit(solution)/shard_map/ppermute | solution.py:357
  183.1 29.0 %collective-permute-start.39 = (bf16[224,768]{1,0:T(8,128)(2,1)}, bf16[224,768]{1,0:T(8,128)(2,1)S(1)}, u32[]{:S(2)}, u32[]{:S(2)}) collective-permute-start(bf16[224,768]{1,0:T(8,128)(2,1)} %pad_maximum_fusion.7), channel_id=1, source_target_pairs={{0,3},{1,0},{2,1},{3,2},{4,7},{5,4},{6,5},{7,6},{8,11},{9,8},{10,9... | collective-permute-start | bytes 1032200 | tf_op jit(solution)/shard_map/ppermute | solution.py:357
  183.5 32.5 %collective-permute-start.31 = (bf16[512,768]{1,0:T(8,128)(2,1)}, bf16[512,768]{1,0:T(8,128)(2,1)S(1)}, u32[]{:S(2)}, u32[]{:S(2)}) collective-permute-start(bf16[512,768]{1,0:T(8,128)(2,1)} %get-tuple-element.132), channel_id=1, source_target_pairs={{0,4},{4,0},{8,12},{12,8},{16,20},{20,16},{24,28},{28,24},{1,5},{5... | collective-permute-start | bytes 2359304 | tf_op jit(solution)/shard_map/ppermute | solution.py:353
  183.5 32.3 %collective-permute-start.44 = (bf16[4,112,576]{2,1,0:T(8,128)(2,1)}, bf16[4,112,576]{2,1,0:T(8,128)(2,1)S(1)}, u32[]{:S(2)}, u32[]{:S(2)}) collective-permute-start(bf16[4,112,576]{2,1,0:T(8,128)(2,1)} %get-tuple-element.151), channel_id=1, source_target_pairs={{0,16},{4,20},{8,24},{12,28},{16,0},{20,4},{24,8},{28,12},{1,17},{... | collective-permute-start | bytes 1548296 | tf_op jit(solution)/shard_map/ppermute | solution.py:353
  212.8 16.9 %collective-permute-start.41 = (bf16[224,768]{1,0:T(8,128)(2,1)S(1)}, bf16[224,768]{1,0:T(8,128)(2,1)S(1)}, u32[]{:S(2)}, u32[]{:S(2)}) collective-permute-start(bf16[224,768]{1,0:T(8,128)(2,1)S(1)} %add_convert_fusion.1.p0), channel_id=1, source_target_pairs={{0,8},{4,12},{8,0},{12,4},{16,24},{20,28},{24,16},{28,20},{1,9},{5... | collective-permute-start | bytes 1032200 | tf_op jit(solution)/shard_map/ppermute | solution.py:353
  214.3 16.3 %collective-permute-start.40 = (bf16[224,768]{1,0:T(8,128)(2,1)S(1)}, bf16[224,768]{1,0:T(8,128)(2,1)S(1)}, u32[]{:S(2)}, u32[]{:S(2)}) collective-permute-start(bf16[224,768]{1,0:T(8,128)(2,1)S(1)} %add_convert_fusion.1.p0), channel_id=1, source_target_pairs={{0,16},{4,20},{8,24},{12,28},{16,0},{20,4},{24,8},{28,12},{1,17},{... | collective-permute-start | bytes 1032200 | tf_op jit(solution)/shard_map/ppermute | solution.py:353
  216.0 14.9 %collective-permute-start.45 = (bf16[112,576]{1,0:T(8,128)(2,1)S(1)}, bf16[112,576]{1,0:T(8,128)(2,1)S(1)}, u32[]{:S(2)}, u32[]{:S(2)}) collective-permute-start(bf16[112,576]{1,0:T(8,128)(2,1)S(1)} %get-tuple-element.163), channel_id=1, source_target_pairs={{0,1},{1,2},{2,3},{3,0},{4,5},{5,6},{6,7},{7,4},{8,9},{9,10},{10,1... | collective-permute-start | bytes 387080 | tf_op jit(solution)/shard_map/ppermute | solution.py:357
  216.0 16.1 %collective-permute-start.47 = (bf16[112,576]{1,0:T(8,128)(2,1)S(1)}, bf16[112,576]{1,0:T(8,128)(2,1)S(1)}, u32[]{:S(2)}, u32[]{:S(2)}) collective-permute-start(bf16[112,576]{1,0:T(8,128)(2,1)S(1)} %get-tuple-element.164), channel_id=1, source_target_pairs={{0,3},{1,0},{2,1},{3,2},{4,7},{5,4},{6,5},{7,6},{8,11},{9,8},{10,9... | collective-permute-start | bytes 387080 | tf_op jit(solution)/shard_map/ppermute | solution.py:357
  230.8 20.4 %collective-permute-start.43 = (bf16[4,224,768]{2,1,0:T(8,128)(2,1)S(1)}, bf16[4,224,768]{2,1,0:T(8,128)(2,1)S(1)}, u32[]{:S(2)}, u32[]{:S(2)}) collective-permute-start(bf16[4,224,768]{2,1,0:T(8,128)(2,1)S(1)} %pad_maximum_fusion), channel_id=1, source_target_pairs={{0,4},{4,0},{8,12},{12,8},{16,20},{20,16},{24,28},{28,24},{1,5},{5... | collective-permute-start | bytes 4128776 | tf_op jit(solution)/shard_map/ppermute | solution.py:353
  (73 other events, 658.6 us)
